TPU v7x, 512 devices: a whole 4x8x8 slice. The times are simulated.
512 devices in a mesh: dp: 64 (over y, z_hi, core), tp: 8 (over z_lo, x).
Axes of the slice: x: 4, y: 8, z: 8 (z_hi: 4, z_lo: 2; z = z_hi * 2 + z_lo), core: 2. Of those that a mesh axis runs over, the one named last changes fastest.
Arguments:
- pool: bfloat16 [4160, 16, 576], P('dp'), may hold values from -4 to 4
- page_table: int32 [320, 13], P('dp'), may hold values from 0 to 256, as said below
- lengths: int32 [320], P('dp'), may hold values from 1 to 208, as said below
- mig_page: int32 [64, 84], P('dp'), may hold values from 0 to 64
- mig_dest: int32 [64, 84], P('dp'), may hold values from 0 to 63, as said below
- queries: bfloat16 [640, 64, 576], P('dp', 'tp'), may hold values from -18 to 18
- new_latent: bfloat16 [640, 576], P('dp'), may hold values from -4 to 4
- w_uv: bfloat16 [64, 512, 128], P('tp'), may hold values from -0.25 to 0.25
- w_out: bfloat16 [8192, 8, 896], P('tp', None, 'dp'), may hold values from -0.0625 to 0.0625
- residual: bfloat16 [640, 8, 896], P(None, 'tp', 'dp'), may hold values from -25 to 25
- norm_gain: bfloat16 [7168], P('tp'), may hold values from 0.5 to 1.5
- w_gate: bfloat16 [7168, 18432], P('tp', 'dp'), may hold values from -0.0625 to 0.0625
- w_up: bfloat16 [7168, 18432], P('tp', 'dp'), may hold values from -0.0625 to 0.0625
- w_down: bfloat16 [18432, 7168], P('dp', 'tp'), may hold values from -0.046875 to 0.046875
Outputs:
- out: bfloat16 [640, 7168], P('dp', 'tp')
Inputs may be any that keep to these rules, and one draw needn't show every extreme that they name: `page_table`: on each rank the entries of the first ceil(lengths/16) slots of its requests name pages that the rank holds after migration (its own, or inbox slots that the migration lists fill); no page is named twice on one rank. `lengths`: some request has exactly 208 cached tokens. `mig_dest`: each rank's list names 28 distinct other ranks, each in 3 consecutive entries.
All inputs are finite; a program needn't handle non-finite values.
Results may differ from a plain program's by a relative error of at most 0.02.
Values may be sent and summed in bfloat16 or wider, within the bound.
A program may use at most 64 MiB of HBM per device.

v0:
```python
import jax
import jax.numpy as jnp
from jax import lax
from jax.sharding import PartitionSpec as P

D = 7168
HD = 128
KVL = 512
ROPE = 64
LAT = 576
PAGE = 16
MAXP = 13
CAP = 3


epsilon = 1e-06


def attend(queries, new_latent, cache_keys, lengths, w_uv):
    requests = cache_keys.shape[0]
    head_count = queries.shape[1]
    score_scale = (HD + ROPE) ** (-0.5)
    query_rows = queries.reshape(requests, 2, head_count, LAT)
    new_rows = new_latent.reshape(requests, 2, LAT)
    cache_scores = (
        jnp.einsum("rqhc,rkc->rqhk", query_rows, cache_keys, preferred_element_type=jnp.float32)
        * score_scale
    )
    position = jnp.arange(cache_keys.shape[1], dtype=jnp.int32)
    live_mask = position[None, :] < lengths[:, None]
    cache_scores = jnp.where(live_mask[:, None, None, :], cache_scores, -jnp.inf)
    new_scores = (
        jnp.einsum("rqhc,rkc->rqhk", query_rows, new_rows, preferred_element_type=jnp.float32)
        * score_scale
    )
    causal_mask = jnp.arange(2)[None, :] <= jnp.arange(2)[:, None]
    new_scores = jnp.where(causal_mask[None, :, None, :], new_scores, -jnp.inf)
    row_max = jnp.maximum(jnp.max(cache_scores, axis=3), jnp.max(new_scores, axis=3))
    cache_exp = jnp.exp(cache_scores - row_max[..., None])
    new_exp = jnp.exp(new_scores - row_max[..., None])
    row_total = jnp.sum(cache_exp, axis=3) + jnp.sum(new_exp, axis=3)
    cache_weights = (cache_exp / row_total[..., None]).astype(jnp.bfloat16)
    new_weights = (new_exp / row_total[..., None]).astype(jnp.bfloat16)
    latent_out = jnp.einsum(
        "rqhk,rkc->rqhc", cache_weights, cache_keys[..., :KVL], preferred_element_type=jnp.float32
    )
    latent_out = latent_out + jnp.einsum(
        "rqhk,rkc->rqhc", new_weights, new_rows[..., :KVL], preferred_element_type=jnp.float32
    )
    latent_out = latent_out.astype(jnp.bfloat16)
    heads_out = jnp.einsum("rqhc,hcd->rqhd", latent_out, w_uv, preferred_element_type=jnp.float32)
    return heads_out.astype(jnp.bfloat16).reshape(2 * requests, head_count * HD)


def local(
    pool,
    page_table,
    lengths,
    mig_page,
    mig_dest,
    queries,
    new_latent,
    w_uv,
    w_out,
    residual,
    norm_gain,
    w_gate,
    w_up,
    w_down,
):
    rank_count = lax.axis_size("dp")
    slot_total = rank_count * CAP
    destination = mig_dest[0]
    page_ids = mig_page[0]
    entry_count = destination.shape[0]
    same_dest = destination[:, None] == destination[None, :]
    earlier = jnp.arange(entry_count)[None, :] < jnp.arange(entry_count)[:, None]
    slot_order = jnp.sum(jnp.logical_and(same_dest, earlier), axis=1)
    target = jnp.where(slot_order < CAP, destination * CAP + slot_order, slot_total)
    slot_match = target[None, :] == jnp.arange(slot_total, dtype=jnp.int32)[:, None]
    source_page = jnp.sum(jnp.where(slot_match, page_ids[None, :], 0), axis=1)
    filled = jnp.any(slot_match, axis=1)
    outgoing = jnp.where(
        filled[:, None, None], jnp.take(pool, source_page, axis=0), jnp.zeros((), pool.dtype)
    )
    outgoing = outgoing.reshape(rank_count, CAP, PAGE, LAT)
    incoming = lax.all_to_all(outgoing, "dp", split_axis=0, concat_axis=0, tiled=True)
    extended = jnp.concatenate([pool, incoming.reshape(slot_total, PAGE, LAT)], axis=0)
    cache_keys = jnp.take(extended, page_table.reshape(-1), axis=0)
    cache_keys = cache_keys.reshape(page_table.shape[0], MAXP * PAGE, LAT)
    heads_out = attend(queries, new_latent, cache_keys, lengths, w_uv)
    w_out_flat = w_out.reshape(w_out.shape[0], w_out.shape[1] * w_out.shape[2])
    projected = jnp.dot(
        lax.all_gather(heads_out, "dp", axis=0, tiled=True),
        w_out_flat,
        preferred_element_type=jnp.float32,
    )
    projected = projected.reshape(projected.shape[0], w_out.shape[1], w_out.shape[2])
    summed = lax.psum_scatter(
        projected.astype(jnp.bfloat16), "tp", scatter_dimension=1, tiled=True
    ).astype(jnp.float32)
    stream = (residual.astype(jnp.float32) + summed).astype(jnp.bfloat16)
    gathered = lax.all_gather(stream, "dp", axis=2, tiled=True)
    gathered = gathered.reshape(gathered.shape[0], gathered.shape[2])
    stream_wide = lax.optimization_barrier(gathered).astype(jnp.float32)
    local_rows = lax.optimization_barrier(stream).astype(jnp.float32)
    squares = lax.psum(jnp.sum(local_rows * local_rows, axis=(1, 2)), ("dp", "tp"))
    scale_rows = lax.rsqrt(squares / D + epsilon)
    normed = (stream_wide * scale_rows[:, None] * norm_gain.astype(jnp.float32)[None, :]).astype(
        jnp.bfloat16
    )
    gate_part = jnp.dot(normed, w_gate, preferred_element_type=jnp.float32)
    up_part = jnp.dot(normed, w_up, preferred_element_type=jnp.float32)
    gate_sum, up_sum = (
        lax.psum(gate_part.astype(jnp.bfloat16), "tp").astype(jnp.float32),
        lax.psum(up_part.astype(jnp.bfloat16), "tp").astype(jnp.float32),
    )
    hidden = (jax.nn.silu(gate_sum) * up_sum).astype(jnp.bfloat16)
    own_rows = hidden.shape[0] // rank_count
    down_sum = lax.psum_scatter(
        jnp.dot(hidden, w_down, preferred_element_type=jnp.float32),
        "dp",
        scatter_dimension=0,
        tiled=True,
    )
    first_row = lax.axis_index("dp") * own_rows
    residual_rows = lax.dynamic_slice_in_dim(stream_wide, first_row, own_rows, 0)
    return (residual_rows + down_sum).astype(jnp.bfloat16)


def solution(mesh):
    in_specs = (
        P("dp", None, None),
        P("dp", None),
        P("dp"),
        P("dp", None),
        P("dp", None),
        P("dp", "tp", None),
        P("dp", None),
        P("tp", None, None),
        P("tp", None, "dp"),
        P(None, "tp", "dp"),
        P("tp"),
        P("tp", "dp"),
        P("tp", "dp"),
        P("dp", "tp"),
    )
    out_specs = P("dp", "tp")
    return jax.shard_map(local, mesh=mesh, in_specs=in_specs, out_specs=out_specs, check_vma=False)
```

profile of v0, /device:TPU:1, one launch (start us, length us, event | category | flops | bytes accessed | tf_op | source)
XLA Modules:
  0.0 1039.5 jit_solution(9459817632049521474)
XLA Ops:
  6.5 0.9 convert_reduce_fusion
  8.2 0.8 select_reduce_fusion
  9.4 4.5 gather_fusion
  13.9 3.8 select_select_fusion
  17.7 17.9 %all-to-all-start = ((bf16[64,3,16,576]{3,2,1,0:T(8,128)(2,1)}), bf16[64,3,16,576]{3,2,1,0:T(8,128)(2,1)}, u32[]{:S(2)}, u32[]{:S(2)}) async-start(bf16[64,3,16,576]{3,2,1,0:T(8,128)(2,1)} %select_select_fusion), calls=%async_computation | async-start | bytes 7864320 | tf_op jit(solution)/shard_map/all_to_all | solution.py:87
  36.6 98.7 %all-to-all-done = bf16[64,3,16,576]{3,2,1,0:T(8,128)(2,1)} async-done(((bf16[64,3,16,576]{3,2,1,0:T(8,128)(2,1)}), bf16[64,3,16,576]{3,2,1,0:T(8,128)(2,1)}, u32[]{:S(2)}, u32[]{:S(2)}) %all-to-all-start) | async-done | bytes 3538976 | tf_op jit(solution)/shard_map/all_to_all | solution.py:87
  135.3 5.2 pad_maximum_fusion
  140.4 3.3 gather_fusion.1
  146.8 93.5 %all-gather.6.cloned.1.call-done = bf16[64,10,1024]{2,1,0:T(8,128)(2,1)} async-done(((bf16[1,10,1024]{2,1,0:T(8,128)(2,1)}), bf16[64,10,1024]{2,1,0:T(8,128)(2,1)}) %all-gather.6.cloned.1.call-update) | async-done | bytes 1310736 | tf_op jit(solution)/shard_map/all_gather | solution.py:94
  240.3 2.6 reshape.167
  242.9 1.2 convolution_convert_fusion.2
  244.2 33.5 %reduce-scatter.3.cloned.1.call-done = bf16[640,1,14]{0,2,1:T(8,128)(2,1)} async-done(((bf16[640,8,14]{0,2,1:T(8,128)(2,1)}), bf16[640,1,14]{0,2,1:T(8,128)(2,1)}) %reduce-scatter.3.cloned.1.call-update) | async-done | bytes 17936 | tf_op jit(solution)/shard_map/reduce_scatter | solution.py:99
  277.7 0.7 add_convert_fusion.1
  279.2 102.2 %psum.21 = f32[640]{0:T(1024)S(1)} all-reduce(f32[640]{0:T(1024)S(1)} %multiply_reduce_fusion), channel_id=1, replica_groups=mesh['dp'=64,'tp'=8] {'dp','tp'}, use_global_device_ids=true, to_apply=%region_9.10 | all-reduce | flops 640 | bytes 5120 | tf_op jit(solution)/shard_map/psum | solution.py:107
  381.4 4.7 copy.38
  386.1 1.5 convolution_convert_fusion.1
  387.7 1.5 convolution_convert_fusion
  389.2 79.1 %all-reduce.7.cloned.1.call-done = (bf16[640,288]{0,1:T(8,128)(2,1)}, bf16[640,288]{0,1:T(8,128)(2,1)}) async-done(((bf16[640,288]{0,1:T(8,128)(2,1)}, bf16[640,288]{0,1:T(8,128)(2,1)}), (bf16[640,288]{0,1:T(8,128)(2,1)}, bf16[640,288]{0,1:T(8,128)(2,1)})) %all-reduce.7.cloned.1.call-update) | async-done | bytes 737296 | tf_op jit(solution)/shard_map/psum | solution.py:116
  468.3 3.5 fusion.21
  471.8 1.3 dynamic-slice
  473.7 1.6 convert_element_type.70
  475.3 554.6 %all-reduce.5.cloned.1.call-done = f32[640,896]{0,1:T(8,128)} async-done(((f32[640,896]{0,1:T(8,128)}), f32[640,896]{0,1:T(8,128)}) %all-reduce.5.cloned.1.call-update) | async-done | bytes 2293776
  1029.9 1.4 constant_dynamic-slice_fusion
  1031.5 1.5 add_convert_fusion
  (72 shorter events, 6.0 us)
Async XLA Ops:
  6.5 138.9 %copy-start = (bf16[8,512,128]{2,1,0:T(8,128)(2,1)S(1)}, bf16[8,512,128]{2,1,0:T(8,128)(2,1)}, u32[]{:S(2)}) copy-start(bf16[8,512,128]{2,1,0:T(8,128)(2,1)} %param.21) | copy-start | bytes 3145732
  17.7 18.0 %copy-start.4 = (bf16[10,576]{1,0:T(8,128)(2,1)S(1)}, bf16[10,576]{1,0:T(8,128)(2,1)}, u32[]{:S(2)}) copy-start(bf16[10,576]{1,0:T(8,128)(2,1)} %param.20) | copy-start | bytes 34564
  17.7 18.1 %copy-start.6 = (s32[5,13]{1,0:T(8,128)S(1)}, s32[5,13]{1,0:T(8,128)}, u32[]{:S(2)}) copy-start(s32[5,13]{1,0:T(8,128)} %param.15) | copy-start | bytes 784
  17.7 18.4 %copy-start.8 = (s32[5]{0:T(128)S(1)}, s32[5]{0:T(128)}, u32[]{:S(2)}) copy-start(s32[5]{0:T(128)} %param.16) | copy-start | bytes 64
  17.7 18.5 %copy-start.3 = (bf16[10,8,576]{2,1,0:T(8,128)(2,1)S(1)}, bf16[10,8,576]{2,1,0:T(8,128)(2,1)}, u32[]{:S(2)}) copy-start(bf16[10,8,576]{2,1,0:T(8,128)(2,1)} %param.19) | copy-start | bytes 276484
  17.7 117.6 %copy-start.1 = (bf16[65,16,576]{2,1,0:T(8,128)(2,1)S(1)}, bf16[65,16,576]{2,1,0:T(8,128)(2,1)}, u32[]{:S(2)}) copy-start(bf16[65,16,576]{2,1,0:T(8,128)(2,1)} %param.14) | copy-start | bytes 3594244
  17.7 117.6 %all-to-all-start = ((bf16[64,3,16,576]{3,2,1,0:T(8,128)(2,1)}), bf16[64,3,16,576]{3,2,1,0:T(8,128)(2,1)}, u32[]{:S(2)}, u32[]{:S(2)}) async-start(bf16[64,3,16,576]{3,2,1,0:T(8,128)(2,1)} %select_select_fusion), calls=%async_computation | async-start | bytes 7864320 | tf_op jit(solution)/shard_map/all_to_all | solution.py:87
  35.7 204.7 %all-gather.6.cloned.1.call-start = ((), (), s32[]{:S(2)}) async-start(), calls=%async_computation.4 | async-start | bytes 2129920 | tf_op jit(solution)/shard_map/all_gather | solution.py:94
  144.0 2.5 copy-start.2
  146.4 131.3 %reduce-scatter.3.cloned.1.call-start = ((), (), s32[]{:S(2)}) async-start(), calls=%async_computation.2 | async-start | bytes 184320 | tf_op jit(solution)/shard_map/reduce_scatter | solution.py:99
  146.8 130.9 %copy-start.5 = (bf16[640,1,14]{0,2,1:T(8,128)(2,1)S(1)}, bf16[640,1,14]{0,2,1:T(8,128)(2,1)}, u32[]{:S(2)}) copy-start(bf16[640,1,14]{0,2,1:T(8,128)(2,1)} %param.23) | copy-start | bytes 53764
  242.9 36.3 %copy-start.7 = (bf16[896]{0:T(1024)(128)(2,1)S(1)}, bf16[896]{0:T(1024)(128)(2,1)}, u32[]{:S(2)}) copy-start(bf16[896]{0:T(1024)(128)(2,1)} %param.24) | copy-start | bytes 5380
  244.1 142.0 %copy-start.9 = (bf16[896,288]{0,1:T(8,128)(2,1)S(1)}, bf16[896,288]{0,1:T(8,128)(2,1)}, u32[]{:S(2)}) copy-start(bf16[896,288]{0,1:T(8,128)(2,1)} %param.25) | copy-start | bytes 1548292
  244.1 137.3 %all-gather.4.cloned.1.call-start = ((), (), s32[]{:S(2)}) async-start(), calls=%async_computation.3 | async-start | bytes 2329600 | tf_op jit(solution)/shard_map/all_gather | solution.py:103
  279.1 189.2 %all-reduce.7.cloned.1.call-start = ((), (), s32[]{:S(2)}) async-start(), calls=%async_computation.6 | async-start | bytes 1474560 | tf_op jit(solution)/shard_map/psum | solution.py:116
  386.1 1.5 copy-start.10
  387.7 80.6 %copy-start.11 = (bf16[288,896]{1,0:T(8,128)(2,1)S(1)}, bf16[288,896]{1,0:T(8,128)(2,1)}, u32[]{:S(2)}) copy-start(bf16[288,896]{1,0:T(8,128)(2,1)} %param.27) | copy-start | bytes 1548292
  389.2 640.8 %all-reduce.5.cloned.1.call-start = ((), (), s32[]{:S(2)}) async-start(), calls=%async_computation.5 | async-start | bytes 4587520
Sparse Core Ops, SparseCore 0:
  146.6 93.7 all-gather.5
  244.2 33.4 reduce-scatter.2
  281.4 89.7 all-gather.3
  389.3 78.9 all-reduce.6
  471.9 557.9 all-reduce.4
where the time goes:
time: 1040 us
  waiting for transfers between devices  860 us (83%)
  blocking collectives  102 us (10%)
  local copies, waits for them, and re-layouts  20 us (2%)
  starting transfers between devices  18.1 us (2%)
  other arithmetic  16 us (2%)
  between operations  14.1 us (1%)
    unnamed x6, waiting for transfers between devices  555 us
    psum x1, blocking collectives, local(): lax.psum(jnp.sum(local_rows * local_rows, axis=(1, 2)), ('dp', 'tp'))  102 us
    all_to_all x1, waiting for transfers between devices, local(): lax.all_to_all(outgoing, 'dp', split_axis=0, concat_axis=0, tiled=True)  98.7 us
    all_gather x1, waiting for transfers between devices, local(): lax.all_gather(heads_out, 'dp', axis=0, tiled=True)  93.5 us
    psum x1, waiting for transfers between devices, local(): lax.psum(up_part.astype(jnp.bfloat16), 'tp').astype(jnp.float32)  79.1 us
    reduce_scatter x1, waiting for transfers between devices, local(): lax.psum_scatter(projected.astype(jnp.bfloat16), 'tp', scatter_dimension=...  33.5 us
  transfers between devices with their start and end apart: 6, of which 5 were waited for; matrix products, arithmetic and copies ran while one was open for 0% of the time, Pallas kernels for 0%

commit v1 on v0

v1 whole, which is shorter than its diff:
```python
import functools

import jax
import jax.numpy as jnp
from jax import lax
from jax.experimental import pallas as pl
from jax.experimental.pallas import tpu as pltpu
from jax.sharding import PartitionSpec as P

D = 7168
HD = 128
KVL = 512
LAT = 576
PAGE = 16
MAXP = 13
REQ = 5
POOL = 65
CAP = 3
NY = 8
NG = 8
NT = 8
KEYS = 32
TOK = 640
EPS = 1e-06
SCALE = 192 ** (-0.5)
BF = jnp.bfloat16
F32 = jnp.float32
MESH = pl.DeviceIdType.MESH
DEAD = -1e30


def dot(a, b, dims):
    return lax.dot_general(a, b, (dims, ((), ())), preferred_element_type=F32)


def iota(shape, axis):
    return lax.broadcasted_iota(jnp.int32, shape, axis)


class Links:
    def __init__(self, send_sems, recv_sems):
        self.send_sems, self.recv_sems, self.used, self.sent = send_sems, recv_sems, 0, []

    def reserve(self, count):
        first = self.used
        self.used += count
        return first

    def copy(self, slot, src, dst, dp, tp):
        return pltpu.make_async_remote_copy(
            src_ref=src,
            dst_ref=dst,
            send_sem=self.send_sems.at[slot],
            recv_sem=self.recv_sems.at[slot],
            device_id={"dp": dp, "tp": tp},
            device_id_type=MESH,
        )

    def send(self, slot, src, dst, dp, tp):
        copy = self.copy(slot, src, dst, dp, tp)
        copy.start()
        self.sent.append(copy)

    def arrived(self, slot, dst, dp, tp):
        self.copy(slot, dst, dst, dp, tp).wait_recv()

    def finish(self):
        for copy in self.sent:
            copy.wait_send()


def ring_gather(links, buf, dp_of, y, core, tp):
    right, left = dp_of(lax.rem(y + 1, NY)), dp_of(lax.rem(y + NY - 1, NY))
    partner = dp_of(y) + 1 - 2 * core
    to_right, to_left, over = links.reserve(4), links.reserve(3), links.reserve(8)

    def pass_on(order, index):
        links.send(over + order, buf.at[core, index], buf.at[core, index], partner, tp)

    links.send(to_right, buf.at[core, y], buf.at[core, y], right, tp)
    links.send(to_left, buf.at[core, y], buf.at[core, y], left, tp)
    pass_on(0, y)
    indices = [y]
    for step in range(4):
        index = lax.rem(y + NY - 1 - step, NY)
        links.arrived(to_right + step, buf.at[core, index], left, tp)
        if step < 3:
            links.send(to_right + step + 1, buf.at[core, index], buf.at[core, index], right, tp)
        pass_on(len(indices), index)
        indices.append(index)
        if step < 3:
            index = lax.rem(y + 1 + step, NY)
            links.arrived(to_left + step, buf.at[core, index], right, tp)
            if step < 2:
                links.send(to_left + step + 1, buf.at[core, index], buf.at[core, index], left, tp)
            pass_on(len(indices), index)
            indices.append(index)
    for order, index in enumerate(indices):
        links.arrived(over + order, buf.at[1 - core, index], partner, tp)


def kernel(
    table, lengths, q, own, inbox, fresh, w_uv, w_out, res, w_gu, w_down, out,
    q_all, keys, o_out, o_in, ho, b_in, heads, pj, c_in, stream, gu, e_in, h_all, part, f_out, f_in,
    acc, r_out, r_in, l_out, l_in, g_out, g_in, send_sems, recv_sems,
):
    dp, t = lax.axis_index("dp"), lax.axis_index("tp")
    y, g = dp // NG, lax.rem(dp, NG)
    z, core = g // 2, lax.rem(g, 2)
    links = Links(send_sems, recv_sems)
    t_to = [lax.rem(t + k, NT) for k in range(NT)]
    t_from = [lax.rem(t + NT - k, NT) for k in range(NT)]
    g_to = [lax.rem(g + k, NG) for k in range(NG)]
    g_from = [lax.rem(g + NG - k, NG) for k in range(NG)]
    z_to = [lax.rem(z + k, 4) for k in range(4)]
    z_from = [lax.rem(z + 4 - k, 4) for k in range(4)]

    def dp_of(yy):
        return yy * NG + g

    def group(gg):
        return y * NG + gg

    barrier = pltpu.get_barrier_semaphore()
    for k in range(1, NT):
        pl.semaphore_signal(barrier, inc=1, device_id={"dp": dp, "tp": t_to[k]}, device_id_type=MESH)
    for k in range(1, NG):
        pl.semaphore_signal(barrier, inc=1, device_id={"dp": group(g_to[k]), "tp": t}, device_id_type=MESH)
    for step in (1, NY - 1):
        pl.semaphore_signal(
            barrier, inc=1, device_id={"dp": dp_of(lax.rem(y + step, NY)), "tp": t}, device_id_type=MESH
        )
    pl.semaphore_wait(barrier, 16)

    slot = links.reserve(NT)
    for k in range(1, NT):
        links.send(slot + k, q, q_all.at[t], dp, t_to[k])
    q_all[t] = q[...]

    def pick(r, carry):
        row = iota((KEYS, 1), 0)
        page = row // 2
        index = jnp.full((KEYS, 1), -1, jnp.int32)
        for k in range(MAXP):
            entry = table[r, k]
            base = jnp.where(entry < POOL, 2 * entry, 1024 + ((entry - POOL) // CAP) * 8 + lax.rem(entry - POOL + CAP, CAP) * 2)
            index = jnp.where(page == k, base + lax.rem(row, 2), index)
        from_own = (index == iota((KEYS, 2 * POOL), 1)).astype(BF)
        from_inbox = (index == iota((KEYS, 512), 1) + 1024).astype(BF)
        from_fresh = (row - 2 * MAXP + 2 * r == iota((KEYS, 2 * REQ), 1)).astype(BF)
        from_fresh = jnp.where(jnp.logical_and(row >= 26, row < 28), from_fresh, jnp.zeros((), BF))
        nn = ((1,), (0,))
        rows = dot(from_own, own[...], nn) + dot(from_inbox, inbox[...], nn) + dot(from_fresh, fresh[...], nn)
        keys[r] = rows.astype(BF)
        return carry

    lax.fori_loop(0, REQ, pick, 0)
    for k in range(1, NT):
        links.arrived(slot + k, q_all.at[t_from[k]], dp, t_from[k])

    def attend(r, carry):
        rows = q_all[:, r].reshape(NT * 16, LAT)
        scores = dot(rows, keys[r], ((1,), (1,))) * SCALE
        row, col = iota((NT * 16, KEYS), 0), iota((NT * 16, KEYS), 1)
        cached = jnp.logical_and(col < 26, (col // 2) * PAGE + 2 * t + lax.rem(col, 2) < lengths[r])
        second = lax.rem(row // 8, 2)
        newer = jnp.logical_and(jnp.logical_and(col >= 26, col <= 26 + second), t == 0)
        live = jnp.logical_or(cached, newer)
        scores = jnp.where(live, scores, DEAD)
        top = jnp.max(scores, axis=1, keepdims=True)
        weights = jnp.where(live, jnp.exp(scores - top), 0.0)
        total = jnp.sum(weights, axis=1, keepdims=True)
        some = total > 0.0
        total = jnp.where(some, total, 1.0)
        latent = dot((weights / total).astype(BF), keys[r][:, :KVL], ((1,), (0,)))
        lse = jnp.where(some, top + jnp.log(total), DEAD)
        high = lse.astype(BF).astype(F32)
        middle = (lse - high).astype(BF).astype(F32)
        low = lse - high - middle
        lane = iota((NT * 16, 128), 1)
        parts = jnp.where(lane == 0, high, jnp.where(lane == 1, middle, jnp.where(lane == 2, low, 0.0)))
        o_out[:, r, :, :KVL] = latent.astype(BF).reshape(NT, 16, KVL)
        o_out[:, r, :, KVL:] = parts.astype(BF).reshape(NT, 16, 128)
        return carry

    lax.fori_loop(0, REQ, attend, 0)
    slot = links.reserve(NT)
    for k in range(1, NT):
        links.send(slot + k, o_out.at[t_to[k]], o_in.at[t], dp, t_to[k])
    o_in[t] = o_out[t]
    for k in range(1, NT):
        links.arrived(slot + k, o_in.at[t_from[k]], dp, t_from[k])
    lse = [jnp.sum(o_in[s, :, :, KVL:].astype(F32), axis=2, keepdims=True) for s in range(NT)]
    top = functools.reduce(jnp.maximum, lse)
    shares = [jnp.exp(v - top) for v in lse]
    total = functools.reduce(jnp.add, shares)
    latent = jnp.zeros((REQ, 16, KVL), F32)
    for s in range(NT):
        latent = latent + o_in[s, :, :, :KVL].astype(F32) * (shares[s] / total)
    latent = latent.astype(BF).reshape(REQ * 16, KVL)

    of_token = (iota((16, 80), 1) // 8 == iota((16, 80), 0)).astype(BF)
    head = lax.rem(iota((80, HD), 0), 8)
    for h in range(8):
        values = jnp.where(head == h, dot(latent, w_uv[h], ((1,), (0,))), 0.0).astype(BF)
        values = dot(of_token, values, ((1,), (0,))).astype(BF)
        ho[h // 4, :, (h % 4) * HD : (h % 4 + 1) * HD] = values

    slot = links.reserve(NG)
    for k in range(1, NG):
        links.send(slot + k, ho.at[lax.rem(g_to[k], 2)], b_in.at[g], group(g_to[k]), t)
    b_in[g] = ho[core]
    for k in range(1, NG):
        links.arrived(slot + k, b_in.at[g_from[k]], group(g_from[k]), t)
    row, col = iota((80, 128), 0), iota((80, 128), 1)
    pack = (col == (row // 10) * 16 + lax.rem(row, 10)).astype(BF)
    heads[core, y] = dot(pack, b_in[...].reshape(128, KVL), ((1,), (0,))).astype(BF)
    ring_gather(links, heads, dp_of, y, core, t)

    nt = ((1,), (1,))
    for half in range(2):
        x = heads[half].reshape(TOK, KVL)
        add = dot(w_out[:, half * KVL : (half + 1) * KVL], x, nt)
        projected = add if half == 0 else projected + add
    pj[...] = projected.astype(BF).reshape(NT, 16, TOK)
    slot = links.reserve(NT)
    for k in range(1, NT):
        links.send(slot + k, pj.at[t_to[k]], c_in.at[t], dp, t_to[k])
    c_in[t] = pj[t]
    for k in range(1, NT):
        links.arrived(slot + k, c_in.at[t_from[k]], dp, t_from[k])
    summed = res[...].astype(F32)
    for s in range(NT):
        summed = summed + c_in[s].astype(F32)
    summed = summed.astype(BF).astype(F32)
    squares = jnp.sum(summed * summed, axis=0, keepdims=True)
    high = squares.astype(BF).astype(F32)
    row = iota((16, TOK), 0)
    piece = jnp.where(row == 14, high, jnp.where(row == 15, squares - high, summed)).astype(BF)
    stream[core, y, z] = piece

    slot = links.reserve(4)
    for k in range(1, 4):
        mine = stream.at[core, y, z]
        links.send(slot + k, mine, mine, group(z_to[k] * 2 + core), t)
    for k in range(1, 4):
        links.arrived(slot + k, stream.at[core, y, z_from[k]], group(z_from[k] * 2 + core), t)
    ring_gather(links, stream, dp_of, y, core, t)

    nn = ((1,), (0,))
    slot = links.reserve(NT)
    columns = stream[...].reshape(1024, TOK)
    for k in range(1, NT + 1):
        to = lax.rem(t + k, NT)
        first = pl.multiple_of(to * 80, 80)
        gu[to] = dot(w_gu[pl.ds(first, 80), :], columns, nn).astype(BF)
        if k < NT:
            links.send(slot + k, gu.at[to], e_in.at[t], dp, to)
        else:
            e_in[t] = gu[t]
    for k in range(1, NT):
        links.arrived(slot + k, e_in.at[t_from[k]], dp, t_from[k])
    total = jnp.zeros((80, TOK), F32)
    for s in range(NT):
        total = total + e_in[s].astype(F32)
    scale = lax.rsqrt(total[36:37] / D + EPS)
    gate, up = total[:40] * scale, total[40:] * scale
    hidden = gate / (1.0 + jnp.exp(-gate)) * up
    hidden = jnp.where(iota((40, TOK), 0) < 36, hidden, 0.0)
    hidden = jnp.concatenate([hidden, jnp.zeros((8, TOK), F32)], axis=0).astype(BF)
    h_all[t] = hidden
    slot = links.reserve(NT)
    for k in range(1, NT):
        links.send(slot + k, h_all.at[t], h_all.at[t], dp, t_to[k])
    for k in range(1, NT):
        links.arrived(slot + k, h_all.at[t_from[k]], dp, t_from[k])

    place = jnp.logical_and(iota((16, 896), 1) == dp * 14 + iota((16, 896), 0), iota((16, 896), 0) < 14).astype(BF)
    tn = ((0,), (0,))
    for block in range(TOK // 128):
        lanes = slice(block * 128, (block + 1) * 128)
        value = dot(h_all[:, :, lanes].reshape(384, 128), w_down[...], tn)
        part[lanes] = value + dot(stream[core, y, z, :, lanes], place, tn)

    partner = dp + 1 - 2 * core
    mine = pl.ds(pl.multiple_of(core * 384, 128), KVL)
    other = pl.ds(pl.multiple_of((1 - core) * 384, 128), KVL)
    f_out[...] = part[:, other].astype(BF)
    slot = links.reserve(1)
    links.send(slot, f_out, f_in, partner, t)
    links.arrived(slot, f_in, partner, t)
    acc[...] = (part[:, mine] + f_in[...].astype(F32)).reshape(NY, 80, KVL)
    right, left = dp_of(lax.rem(y + 1, NY)), dp_of(lax.rem(y + NY - 1, NY))
    to_right, to_left = links.reserve(4), links.reserve(3)
    for step in range(4):
        value = acc[lax.rem(y + 4 - step, NY)]
        if step > 0:
            links.arrived(to_right + step - 1, r_in.at[step - 1], left, t)
            value = value + r_in[step - 1].astype(F32)
        r_out[step] = value.astype(BF)
        links.send(to_right + step, r_out.at[step], r_in.at[step], right, t)
        if step < 3:
            value = acc[lax.rem(y + NY - 3 + step, NY)]
            if step > 0:
                links.arrived(to_left + step - 1, l_in.at[step - 1], right, t)
                value = value + l_in[step - 1].astype(F32)
            l_out[step] = value.astype(BF)
            links.send(to_left + step, l_out.at[step], l_in.at[step], left, t)
    links.arrived(to_right + 3, r_in.at[3], left, t)
    links.arrived(to_left + 2, l_in.at[2], right, t)
    value = (acc[y] + r_in[3].astype(F32) + l_in[2].astype(F32)).astype(BF)
    row, col = iota((128, 80), 0), iota((128, 80), 1)
    spread = jnp.logical_and(lax.rem(row, 16) < 10, col == (row // 16) * 10 + lax.rem(row, 16)).astype(BF)
    g_out[...] = dot(spread, value, nn).astype(BF).reshape(NG, 16, KVL)
    slot = links.reserve(NG)
    for k in range(1, NG):
        links.send(slot + k, g_out.at[g_to[k]], g_in.at[g], group(g_to[k]), t)
    g_in[g] = g_out[g]
    for k in range(1, NG):
        links.arrived(slot + k, g_in.at[g_from[k]], group(g_from[k]), t)
    first = jnp.zeros((16, KVL), F32)
    second = jnp.zeros((16, KVL), F32)
    for s in range(4):
        first = first + g_in[2 * s].astype(F32)
        second = second + g_in[2 * s + 1].astype(F32)
    out[:, :KVL] = first.astype(BF)[:10]
    out[:, KVL:] = second.astype(BF)[:10, 128:]
    links.finish()


SLOTS = 8 * 7 + 2 * 15 + 4 + 8


def layer(*operands):
    scratch = [
        ((NT, REQ, 16, LAT), BF),
        ((REQ, KEYS, LAT), BF),
        ((NT, REQ, 16, 640), BF),
        ((NT, REQ, 16, 640), BF),
        ((2, 16, KVL), BF),
        ((NG, 16, KVL), BF),
        ((2, NY, 80, KVL), BF),
        ((NT, 16, TOK), BF),
        ((NT, 16, TOK), BF),
        ((2, NY, 4, 16, TOK), BF),
        ((NT, 80, TOK), BF),
        ((NT, 80, TOK), BF),
        ((NT, 48, TOK), BF),
        ((TOK, 896), F32),
        ((TOK, KVL), BF),
        ((TOK, KVL), BF),
        ((NY, 80, KVL), F32),
        ((4, 80, KVL), BF),
        ((4, 80, KVL), BF),
        ((3, 80, KVL), BF),
        ((3, 80, KVL), BF),
        ((NG, 16, KVL), BF),
        ((NG, 16, KVL), BF),
    ]
    smem = pl.BlockSpec(memory_space=pltpu.SMEM)
    vmem = pl.BlockSpec(memory_space=pltpu.VMEM)
    return pl.pallas_call(
        kernel,
        out_shape=jax.ShapeDtypeStruct((10, 896), BF),
        in_specs=[smem] * 2 + [vmem] * 9,
        out_specs=vmem,
        scratch_shapes=[pltpu.VMEM(shape, kind) for shape, kind in scratch]
        + [pltpu.SemaphoreType.DMA((SLOTS,)), pltpu.SemaphoreType.DMA((SLOTS,))],
        compiler_params=pltpu.CompilerParams(
            collective_id=0, has_side_effects=True, vmem_limit_bytes=48 * 1024 * 1024
        ),
        cost_estimate=pl.CostEstimate(flops=3 * 10**9, bytes_accessed=10**7, transcendentals=10**6),
        name="layer",
    )(*operands)


def local(
    pool,
    page_table,
    lengths,
    mig_page,
    mig_dest,
    queries,
    new_latent,
    w_uv,
    w_out,
    residual,
    norm_gain,
    w_gate,
    w_up,
    w_down,
):
    t = lax.axis_index("tp")
    own = lax.dynamic_slice(pool, (0, 2 * t, 0), (POOL, 2, LAT)).reshape(2 * POOL, LAT)
    order = jnp.arange(CAP * 28, dtype=jnp.int32) % CAP
    row = jnp.arange(512, dtype=jnp.int32)
    match = jnp.logical_and(
        mig_dest[0][None, :] == (row // 8)[:, None], order[None, :] == ((row % 8) // 2)[:, None]
    )
    source = jnp.sum(jnp.where(match, 2 * mig_page[0][None, :] + 1 + (row % 2)[:, None], 0), axis=1) - 1
    select = (source[:, None] == jnp.arange(2 * POOL, dtype=jnp.int32)[None, :]).astype(BF)
    outgoing = jnp.dot(select, own, preferred_element_type=F32).astype(BF).reshape(64, 8, LAT)
    inbox = lax.all_to_all(outgoing, "dp", split_axis=0, concat_axis=0, tiled=True).reshape(512, LAT)

    gain = norm_gain.astype(F32)[:, None]

    def widen(w):
        w = (w.astype(F32) * gain).astype(BF).reshape(64, 14, NT, 36)
        return jnp.pad(w, ((0, 0), (0, 2), (0, 0), (0, 4)))

    w_gu = jnp.stack([widen(w_gate), widen(w_up)], axis=3)
    inner, slot = jnp.arange(16)[:, None], jnp.arange(80)[None, :]
    ones = jnp.logical_and(inner >= 14, slot == 36).reshape(1, 16, 1, 2, 40)
    w_gu = jnp.where(ones, jnp.ones((), BF), w_gu)
    w_gu = w_gu.reshape(NY, 4, 2, 16, TOK).transpose(4, 2, 0, 1, 3).reshape(TOK, 1024)
    w_out_t = jnp.pad(w_out, ((0, 0), (0, 0), (0, 2))).reshape(1024, 128).T
    res_t = jnp.pad(residual.reshape(TOK, 14).T, ((0, 2), (0, 0)))
    w_down_p = jnp.pad(w_down.reshape(NT, 36, 896), ((0, 0), (0, 12), (0, 0))).reshape(384, 896)
    q = queries.reshape(REQ, 16, LAT)
    return layer(page_table, lengths, q, own, inbox, new_latent, w_uv, w_out_t, res_t, w_gu, w_down_p)


def solution(mesh):
    in_specs = (
        P("dp", None, None),
        P("dp", None),
        P("dp"),
        P("dp", None),
        P("dp", None),
        P("dp", "tp", None),
        P("dp", None),
        P("tp", None, None),
        P("tp", None, "dp"),
        P(None, "tp", "dp"),
        P("tp"),
        P("tp", "dp"),
        P("tp", "dp"),
        P("dp", "tp"),
    )
    out_specs = P("dp", "tp")
    return jax.shard_map(local, mesh=mesh, in_specs=in_specs, out_specs=out_specs, check_vma=False)
```

time: 1040 us -> 204 us (0.20)
  waiting for transfers between devices: 860 us -> 0.01 us
  Pallas kernels: 0 us -> 133 us
  blocking collectives: 102 us -> 0 us
  local copies, waits for them, and re-layouts: 20 us -> 47.8 us
  between operations: 14.1 us -> 0.28 us
  other arithmetic: 16 us -> 3.66 us
    unnamed x6 -> x0, waiting for transfers between devices: 555 us -> none
    pallas_call x0 -> x1, Pallas kernels: none -> 133 us  [layer(): pl.pallas_call(kernel, out_shape=jax.ShapeDtypeStruct((10, 896), BF), in_...]
    psum x1 -> x0, blocking collectives: 102 us -> none  [local(): lax.psum(jnp.sum(local_rows * local_rows, axis=(1, 2)), ('dp', 'tp'))]
    all_to_all x1, waiting for transfers between devices: 98.7 us -> 0.01 us  [local(): lax.all_to_all(outgoing, 'dp', split_axis=0, concat_axis=0, tiled=True)]
    all_gather x2 -> x0, waiting for transfers between devices: 93.5 us -> none  [the longest x1 93.5 us: local(): lax.all_gather(heads_out, 'dp', axis=0, tiled=True)]
    psum x1 -> x0, waiting for transfers between devices: 79.1 us -> none  [local(): lax.psum(up_part.astype(jnp.bfloat16), 'tp').astype(jnp.float32)]
    reduce_scatter x1 -> x0, waiting for transfers between devices: 33.5 us -> none  [local(): lax.psum_scatter(projected.astype(jnp.bfloat16), 'tp', scatter_dimension=...]
    another operation x0 -> x3, local copies, waits for them, and re-layouts: none -> 24.3 us  [local(): w_gu = jnp.stack([widen(w_gate), widen(w_up)], axis=3)]
  transfers between devices with their start and end apart: 6 -> 1, of which waited for: 5 -> 0; matrix products, arithmetic and copies ran while one was open for 0% -> 21% of each run, Pallas kernels for 0% -> 0%
where the time goes in v1:
time: 204 us; the launch traced here: 203 us
  Pallas kernels  133 us (65%)
  local copies, waits for them, and re-layouts  47.8 us (23%)
  starting transfers between devices  17.8 us (9%)
  other arithmetic  3.66 us (2%)
    pallas_call x1, Pallas kernels, layer(): pl.pallas_call(kernel, out_shape=jax.ShapeDtypeStruct((10, 896), BF), in_...  133 us
    another operation x3, local copies, waits for them, and re-layouts, local(): w_gu = jnp.stack([widen(w_gate), widen(w_up)], axis=3)  24.3 us
    all_to_all x1, starting transfers between devices, local(): lax.all_to_all(outgoing, 'dp', split_axis=0, concat_axis=0, tiled=True)  17.8 us
    reshape x2, local copies, waits for them, and re-layouts, widen(): w = (w.astype(F32) * gain).astype(BF).reshape(64, 14, NT, 36)  6.62 us
    unnamed x26, local copies, waits for them, and re-layouts  6.08 us
  transfers between devices with their start and end apart: 1, of which 0 were waited for; matrix products, arithmetic and copies ran while one was open for 21% of the time, Pallas kernels for 0%

profile of v1, /device:TPU:1, one launch (start us, length us, event | category | flops | bytes accessed | tf_op | source)
XLA Modules:
  0.0 203.5 jit_solution(15189114202272405702)
XLA Ops:
  0.0 1.3 copy-done
  1.8 0.7 add_bitcast_fusion
  2.5 0.8 select_reduce_fusion
  3.8 1.1 copy.31
  4.9 17.8 %all-to-all-start = ((bf16[64,8,576]{2,1,0:T(8,128)(2,1)}), bf16[64,8,576]{2,1,0:T(8,128)(2,1)}, u32[]{:S(2)}, u32[]{:S(2)}) async-start(bf16[64,8,576]{2,1,0:T(8,128)(2,1)} %bitcast.3), calls=%async_computation | async-start | bytes 1310720 | tf_op jit(solution)/shard_map/all_to_all | solution.py:403
  22.7 1.0 multiply_convert_fusion.1
  23.7 1.1 copy.33
  24.9 2.9 %reshape.127 = bf16[64,14,8,36]{3,2,1,0:T(8,128)(2,1)S(1)} reshape(bf16[896,288]{1,0:T(8,128)(2,1)} %copy.33) | data formatting | bytes 1032192 | tf_op jit(solution)/shard_map/reshape | solution.py:408
  27.7 2.2 %copy.34 = bf16[896,288]{1,0:T(8,128)(2,1)} copy(bf16[896,288]{0,1:T(8,128)(2,1)} %get-tuple-element.6) | data formatting | bytes 1032192 | tf_op jit(solution)/shard_map/convert_element_type | solution.py:408
  29.9 3.7 %reshape.128 = bf16[64,14,8,36]{3,2,1,0:T(8,128)(2,1)} reshape(bf16[896,288]{1,0:T(8,128)(2,1)} %copy.34) | data formatting | bytes 1032192 | tf_op jit(solution)/shard_map/reshape | solution.py:408
  33.7 2.7 %pad_bitcast_fusion = (bf16[64,16,8,1,40]{4,2,1,0,3:T(8,128)(2,1)S(1)}, bf16[64,16,8,1,40]{4,2,1,0,3:T(8,128)(2,1)S(1)}) fusion(bf16[64,14,8,36]{3,2,1,0:T(8,128)(2,1)} %reshape.128, bf16[64,14,8,36]{3,2,1,0:T(8,128)(2,1)S(1)} %reshape.127), kind=kLoop, calls=%fused_computation.1 | loop fusion | bytes 2342912 | tf_op jit(solution)/shard_map/stack | solution.py:411
  36.4 0.9 pad_maximum_fusion
  37.3 9.7 %copy.35 = bf16[64,16,8,2,40]{4,3,2,1,0:T(2,128)(2,1)} copy(bf16[64,16,8,2,40]{4,2,1,0,3:T(8,128)(2,1)S(1)} %pad_maximum_fusion) | data formatting | bytes 2621440 | tf_op jit(solution)/shard_map/stack | solution.py:411
  47.1 11.9 %stack.14 = bf16[8,4,2,16,640]{4,3,2,1,0:T(8,128)(2,1)S(1)} reshape(bf16[64,16,8,2,40]{4,3,2,1,0:T(2,128)(2,1)} %copy.35) | data formatting | bytes 2621440 | tf_op jit(solution)/shard_map/stack | solution.py:411
  59.4 1.3 copy.36
  60.7 1.7 copy.37.w_gu
  62.4 0.9 reshape.130
  63.3 1.1 copy.38
  64.4 1.1 pad.23
  65.5 0.7 pad.19.clone
  66.3 0.9 copy-done.1
  67.3 1.2 copy-done.2
  68.5 0.9 copy-done.3
  69.4 133.5 %layer.1 = bf16[10,896]{1,0:T(8,128)(2,1)S(1)} custom-call(s32[5,13]{1,0:T(8,128)S(1)} %copy-done.5, s32[5]{0:T(128)S(1)} %copy-done.6, bf16[5,16,576]{2,1,0:T(8,128)(2,1)S(1)} %bitcast.23, bf16[130,576]{1,0:T(8,128)(2,1)S(1)} %reshape.122.own, bf16[512,576]{1,0:T(8,128)(2,1)} %bitcast.4.inbox, bf16[10,576]{1,0:T(8,128)(2,1)S(1)} %copy-done.4, ...), custom_call_target="tpu_custom_call" | custom-call | flops 3000000000 | bytes 10000000 | tf_op jit(solution)/shard_map/layer/pallas_call | solution.py:362
  (37 shorter events, 2.1 us)
Async XLA Ops:
  0.0 1.3 copy-start
  1.5 21.2 %copy-start.11 = (bf16[896]{0:T(1024)(128)(2,1)S(1)}, bf16[896]{0:T(1024)(128)(2,1)}, u32[]{:S(2)}) copy-start(bf16[896]{0:T(1024)(128)(2,1)} %param.24) | copy-start | bytes 5380
  1.5 21.2 %copy-start.7 = (bf16[896,288]{0,1:T(8,128)(2,1)S(1)}, bf16[896,288]{0,1:T(8,128)(2,1)}, u32[]{:S(2)}) copy-start(bf16[896,288]{0,1:T(8,128)(2,1)} %param.25) | copy-start | bytes 1548292
  1.5 21.2 %copy-start.8 = (bf16[896,288]{0,1:T(8,128)(2,1)S(1)}, bf16[896,288]{0,1:T(8,128)(2,1)}, u32[]{:S(2)}) copy-start(bf16[896,288]{0,1:T(8,128)(2,1)} %param.26) | copy-start | bytes 1548292
  4.9 61.4 %all-to-all-start = ((bf16[64,8,576]{2,1,0:T(8,128)(2,1)}), bf16[64,8,576]{2,1,0:T(8,128)(2,1)}, u32[]{:S(2)}, u32[]{:S(2)}) async-start(bf16[64,8,576]{2,1,0:T(8,128)(2,1)} %bitcast.3), calls=%async_computation | async-start | bytes 1310720 | tf_op jit(solution)/shard_map/all_to_all | solution.py:403
  60.7 1.7 copy-start.9
  62.4 3.9 %copy-start.4 = (bf16[10,576]{1,0:T(8,128)(2,1)S(1)}, bf16[10,576]{1,0:T(8,128)(2,1)}, u32[]{:S(2)}) copy-start(bf16[10,576]{1,0:T(8,128)(2,1)} %fresh.1) | copy-start | bytes 34564
  62.4 3.9 %copy-start.5 = (s32[5,13]{1,0:T(8,128)S(1)}, s32[5,13]{1,0:T(8,128)}, u32[]{:S(2)}) copy-start(s32[5,13]{1,0:T(8,128)} %table.1) | copy-start | bytes 784
  62.4 3.9 %copy-start.6 = (s32[5]{0:T(128)S(1)}, s32[5]{0:T(128)}, u32[]{:S(2)}) copy-start(s32[5]{0:T(128)} %lengths.1) | copy-start | bytes 64
  63.3 2.9 %copy-start.10 = (bf16[640,1,14]{0,2,1:T(8,128)(2,1)S(1)}, bf16[640,1,14]{0,2,1:T(8,128)(2,1)}, u32[]{:S(2)}) copy-start(bf16[640,1,14]{0,2,1:T(8,128)(2,1)} %param.23) | copy-start | bytes 53764
  66.3 1.0 copy-start.1
  67.3 1.2 copy-start.2
  68.5 0.9 copy-start.3

commit v2 on v1

--- a/solution.py
+++ b/solution.py
@@ -100,7 +100,8 @@
 
 
 def kernel(
-    table, lengths, q, own, inbox, fresh, w_uv, w_out, res, w_gu, w_down, out,
+    table, lengths, mig_page, mig_dest, q, pool, fresh, w_uv, w_out, res, gain, w_gate, w_up, w_down, out,
+    own, a_y1, a_y2, a_y3, a_y4, a_z1, a_z2, a_z3, a_z4, w_gu, w_o, w_d,
     q_all, keys, o_out, o_in, ho, b_in, heads, pj, c_in, stream, gu, e_in, h_all, part, f_out, f_in,
     acc, r_out, r_in, l_out, l_in, g_out, g_in, send_sems, recv_sems,
 ):
@@ -112,8 +113,11 @@
     t_from = [lax.rem(t + NT - k, NT) for k in range(NT)]
     g_to = [lax.rem(g + k, NG) for k in range(NG)]
     g_from = [lax.rem(g + NG - k, NG) for k in range(NG)]
+    y_to = [lax.rem(y + k, NY) for k in range(NY)]
+    y_from = [lax.rem(y + NY - k, NY) for k in range(NY)]
     z_to = [lax.rem(z + k, 4) for k in range(4)]
     z_from = [lax.rem(z + 4 - k, 4) for k in range(4)]
+    nn, nt, tn = ((1,), (0,)), ((1,), (1,)), ((0,), (0,))
 
     def dp_of(yy):
         return yy * NG + g
@@ -126,64 +130,131 @@
         pl.semaphore_signal(barrier, inc=1, device_id={"dp": dp, "tp": t_to[k]}, device_id_type=MESH)
     for k in range(1, NG):
         pl.semaphore_signal(barrier, inc=1, device_id={"dp": group(g_to[k]), "tp": t}, device_id_type=MESH)
-    for step in (1, NY - 1):
-        pl.semaphore_signal(
-            barrier, inc=1, device_id={"dp": dp_of(lax.rem(y + step, NY)), "tp": t}, device_id_type=MESH
-        )
-    pl.semaphore_wait(barrier, 16)
-
-    slot = links.reserve(NT)
-    for k in range(1, NT):
-        links.send(slot + k, q, q_all.at[t], dp, t_to[k])
+    for k in range(1, NY):
+        pl.semaphore_signal(barrier, inc=1, device_id={"dp": dp_of(y_to[k]), "tp": t}, device_id_type=MESH)
+
+    row = iota((144, 1), 0)
+    column = (row // 2) * PAGE + 2 * t + lax.rem(row, 2)
+    own[...] = dot((column == iota((144, POOL * PAGE), 1)).astype(BF), pool[...], nn).astype(BF)
+    row = iota((384, 1), 0)
+    inner = lax.rem(row, 6)
+    entry = lax.rem(iota((1, CAP * 28), 1), CAP)
+
+    def outgoing(rank):
+        match = jnp.logical_and(mig_dest[...] == rank, entry == inner // 2)
+        source = jnp.sum(jnp.where(match, (mig_page[...] + 1).astype(F32), 0.0), axis=1, keepdims=True)
+        source = source.astype(jnp.int32) * 2 - 2 + lax.rem(inner, 2)
+        return (source == iota((384, 144), 1)).astype(BF)
+
+    first, second = row // 48, lax.rem(row, 48) // 6
+    a_y1[...] = dot(outgoing(first * NG + second), own[:, :384], nn).astype(BF).reshape(NY, 48, 384)
+    a_z1[...] = dot(outgoing(second * NG + first), own[:, 384:], nn).astype(BF).reshape(NG, 48, 192)
     q_all[t] = q[...]
 
-    def pick(r, carry):
-        row = iota((KEYS, 1), 0)
-        page = row // 2
-        index = jnp.full((KEYS, 1), -1, jnp.int32)
+    pl.semaphore_wait(barrier, 21)
+    along_y, along_g = links.reserve(NY), links.reserve(NG)
+    for k in range(1, NY):
+        links.send(along_y + k, a_y1.at[y_to[k]], a_y2.at[y], dp_of(y_to[k]), t)
+        links.send(along_g + k, a_z1.at[g_to[k]], a_z2.at[g], group(g_to[k]), t)
+    to_heads = links.reserve(NT)
+    for k in range(1, NT):
+        links.send(to_heads + k, q_all.at[t], q_all.at[t], dp, t_to[k])
+    a_y2[y] = a_y1[y]
+    a_z2[g] = a_z1[g]
+
+    row, col = iota((128, 1), 0), iota((128, 112), 1)
+    spread = jnp.logical_and(lax.rem(row, 16) < 14, col == lax.rem(row, 16) * 8 + row // 16).astype(BF)
+    w_o[...] = dot(spread, w_out[...], nn).astype(BF)
+    row, col = iota((384, 1), 0), iota((384, 288), 1)
+    spread = jnp.logical_and(lax.rem(row, 48) < 36, col == (row // 48) * 36 + lax.rem(row, 48)).astype(BF)
+    w_d[...] = dot(spread, w_down[...], nn).astype(BF)
+
+    for k in range(1, NY):
+        links.arrived(along_y + k, a_y2.at[y_from[k]], dp_of(y_from[k]), t)
+        links.arrived(along_g + k, a_z2.at[g_from[k]], group(g_from[k]), t)
+    row, col = iota((384, 1), 0), iota((384, 384), 1)
+    swap = (col == (lax.rem(row, 48) // 6) * 48 + (row // 48) * 6 + lax.rem(row, 6)).astype(BF)
+    a_y3[...] = dot(swap, a_y2[...].reshape(384, 384), nn).astype(BF).reshape(NG, 48, 384)
+    a_z3[...] = dot(swap, a_z2[...].reshape(384, 192), nn).astype(BF).reshape(NY, 48, 192)
+    along_g, along_y = links.reserve(NG), links.reserve(NY)
+    for k in range(1, NY):
+        links.send(along_g + k, a_y3.at[g_to[k]], a_y4.at[g], group(g_to[k]), t)
+        links.send(along_y + k, a_z3.at[y_to[k]], a_z4.at[y], dp_of(y_to[k]), t)
+    a_y4[g] = a_y3[g]
+    a_z4[y] = a_z3[y]
+
+    row, col = iota((NT * 80, 1), 0), iota((NT * 80, 288), 1)
+    slot = lax.rem(row, 80)
+    of_gate = jnp.logical_and(slot < 36, col == (row // 80) * 36 + slot).astype(BF)
+    of_up = jnp.logical_and(jnp.logical_and(slot >= 40, slot < 76), col == (row // 80) * 36 + slot - 40).astype(BF)
+    scale = gain[...].astype(F32)
+    rows = dot(of_gate, (w_gate[...].astype(F32) * scale).astype(BF), nn)
+    rows = (rows + dot(of_up, (w_up[...].astype(F32) * scale).astype(BF), nn)).astype(BF)
+    row, col = iota((896, 1), 0), iota((896, 1024), 1)
+    rank = row // 14
+    at = lax.rem(rank, 2) * 512 + (rank // 2) * 16 + lax.rem(row, 14)
+    spread = (col == at).astype(BF)
+    squares_at = jnp.logical_and(lax.rem(iota((NT * 80, 1), 0), 80) == 36, lax.rem(iota((1, 1024), 1), 16) >= 14)
+    w_gu[...] = jnp.where(squares_at, 1.0, dot(rows, spread, nn)).astype(BF)
+
+    for k in range(1, NY):
+        links.arrived(along_g + k, a_y4.at[g_from[k]], group(g_from[k]), t)
+        links.arrived(along_y + k, a_z4.at[y_from[k]], dp_of(y_from[k]), t)
+
+    row = iota((REQ * KEYS, 1), 0)
+    place, request = lax.rem(row, KEYS), row // KEYS
+    named = jnp.full((REQ * KEYS, 1), -1, jnp.int32)
+    for r in range(REQ):
         for k in range(MAXP):
-            entry = table[r, k]
-            base = jnp.where(entry < POOL, 2 * entry, 1024 + ((entry - POOL) // CAP) * 8 + lax.rem(entry - POOL + CAP, CAP) * 2)
-            index = jnp.where(page == k, base + lax.rem(row, 2), index)
-        from_own = (index == iota((KEYS, 2 * POOL), 1)).astype(BF)
-        from_inbox = (index == iota((KEYS, 512), 1) + 1024).astype(BF)
-        from_fresh = (row - 2 * MAXP + 2 * r == iota((KEYS, 2 * REQ), 1)).astype(BF)
-        from_fresh = jnp.where(jnp.logical_and(row >= 26, row < 28), from_fresh, jnp.zeros((), BF))
-        nn = ((1,), (0,))
-        rows = dot(from_own, own[...], nn) + dot(from_inbox, inbox[...], nn) + dot(from_fresh, fresh[...], nn)
-        keys[r] = rows.astype(BF)
-        return carry
-
-    lax.fori_loop(0, REQ, pick, 0)
-    for k in range(1, NT):
-        links.arrived(slot + k, q_all.at[t_from[k]], dp, t_from[k])
-
-    def attend(r, carry):
-        rows = q_all[:, r].reshape(NT * 16, LAT)
-        scores = dot(rows, keys[r], ((1,), (1,))) * SCALE
-        row, col = iota((NT * 16, KEYS), 0), iota((NT * 16, KEYS), 1)
-        cached = jnp.logical_and(col < 26, (col // 2) * PAGE + 2 * t + lax.rem(col, 2) < lengths[r])
-        second = lax.rem(row // 8, 2)
-        newer = jnp.logical_and(jnp.logical_and(col >= 26, col <= 26 + second), t == 0)
-        live = jnp.logical_or(cached, newer)
-        scores = jnp.where(live, scores, DEAD)
-        top = jnp.max(scores, axis=1, keepdims=True)
-        weights = jnp.where(live, jnp.exp(scores - top), 0.0)
-        total = jnp.sum(weights, axis=1, keepdims=True)
-        some = total > 0.0
-        total = jnp.where(some, total, 1.0)
-        latent = dot((weights / total).astype(BF), keys[r][:, :KVL], ((1,), (0,)))
-        lse = jnp.where(some, top + jnp.log(total), DEAD)
-        high = lse.astype(BF).astype(F32)
-        middle = (lse - high).astype(BF).astype(F32)
-        low = lse - high - middle
-        lane = iota((NT * 16, 128), 1)
-        parts = jnp.where(lane == 0, high, jnp.where(lane == 1, middle, jnp.where(lane == 2, low, 0.0)))
+            named = jnp.where(jnp.logical_and(request == r, place // 2 == k), table[r, k], named)
+    token = lax.rem(place, 2)
+    from_own = (jnp.where(jnp.logical_and(named >= 0, named < POOL), 2 * named + token, -1) == iota((REQ * KEYS, 144), 1)).astype(BF)
+    migrated = jnp.maximum(named - POOL, 0)
+    rank = (migrated * 171) // 512
+    inner = (migrated - CAP * rank) * 2 + token
+    rank_y, rank_g = rank // NG, lax.rem(rank, NG)
+    in_inbox = named >= POOL
+    at = jnp.where(in_inbox, rank_g * 48 + rank_y * 6 + inner, -1)
+    from_y = (at == iota((REQ * KEYS, 384), 1)).astype(BF)
+    at = jnp.where(in_inbox, rank_y * 48 + rank_g * 6 + inner, -1)
+    from_z = (at == iota((REQ * KEYS, 384), 1)).astype(BF)
+    at = jnp.where(jnp.logical_and(place >= 26, place < 28), 2 * request + place - 26, -1)
+    from_fresh = (at == iota((REQ * KEYS, 2 * REQ), 1)).astype(BF)
+    low = dot(from_own, own[:, :384], nn) + dot(from_fresh, fresh[:, :384], nn)
+    high = dot(from_own, own[:, 384:], nn) + dot(from_fresh, fresh[:, 384:], nn)
+    low = low + dot(from_y, a_y4[...].reshape(384, 384), nn)
+    high = high + dot(from_z, a_z4[...].reshape(384, 192), nn)
+    keys[:, :, :384] = low.astype(BF).reshape(REQ, KEYS, 384)
+    keys[:, :, 384:] = high.astype(BF).reshape(REQ, KEYS, 192)
+    for k in range(1, NT):
+        links.arrived(to_heads + k, q_all.at[t_from[k]], dp, t_from[k])
+
+    scores = [dot(q_all[:, r].reshape(NT * 16, LAT), keys[r], nt) for r in range(REQ)]
+    scores = jnp.concatenate(scores, axis=0) * SCALE
+    row, col = iota((REQ * 128, 1), 0), iota((REQ * 128, KEYS), 1)
+    length = jnp.full((REQ * 128, 1), lengths[0], jnp.int32)
+    for r in range(1, REQ):
+        length = jnp.where(row >= r * 128, lengths[r], length)
+    cached = jnp.logical_and(col < 26, (col // 2) * PAGE + 2 * t + lax.rem(col, 2) < length)
+    newer = jnp.logical_and(jnp.logical_and(col >= 26, col <= 26 + lax.rem(row // 8, 2)), t == 0)
+    live = jnp.logical_or(cached, newer)
+    scores = jnp.where(live, scores, DEAD)
+    top = jnp.max(scores, axis=1, keepdims=True)
+    weights = jnp.where(live, jnp.exp(scores - top), 0.0)
+    total = jnp.sum(weights, axis=1, keepdims=True)
+    some = total > 0.0
+    total = jnp.where(some, total, 1.0)
+    weights = (weights / total).astype(BF)
+    lse = jnp.where(some, top + jnp.log(total), DEAD)
+    high = lse.astype(BF).astype(F32)
+    middle = (lse - high).astype(BF).astype(F32)
+    low = lse - high - middle
+    lane = iota((REQ * 128, 128), 1)
+    parts = jnp.where(lane == 0, high, jnp.where(lane == 1, middle, jnp.where(lane == 2, low, 0.0))).astype(BF)
+    for r in range(REQ):
+        latent = dot(weights[r * 128 : (r + 1) * 128], keys[r][:, :KVL], nn)
         o_out[:, r, :, :KVL] = latent.astype(BF).reshape(NT, 16, KVL)
-        o_out[:, r, :, KVL:] = parts.astype(BF).reshape(NT, 16, 128)
-        return carry
-
-    lax.fori_loop(0, REQ, attend, 0)
+        o_out[:, r, :, KVL:] = parts[r * 128 : (r + 1) * 128].reshape(NT, 16, 128)
     slot = links.reserve(NT)
     for k in range(1, NT):
         links.send(slot + k, o_out.at[t_to[k]], o_in.at[t], dp, t_to[k])
@@ -212,15 +283,14 @@
     b_in[g] = ho[core]
     for k in range(1, NG):
         links.arrived(slot + k, b_in.at[g_from[k]], group(g_from[k]), t)
-    row, col = iota((80, 128), 0), iota((80, 128), 1)
+    row, col = iota((80, 1), 0), iota((80, 128), 1)
     pack = (col == (row // 10) * 16 + lax.rem(row, 10)).astype(BF)
     heads[core, y] = dot(pack, b_in[...].reshape(128, KVL), ((1,), (0,))).astype(BF)
     ring_gather(links, heads, dp_of, y, core, t)
 
-    nt = ((1,), (1,))
     for half in range(2):
         x = heads[half].reshape(TOK, KVL)
-        add = dot(w_out[:, half * KVL : (half + 1) * KVL], x, nt)
+        add = dot(w_o[:, half * KVL : (half + 1) * KVL], x, nt)
         projected = add if half == 0 else projected + add
     pj[...] = projected.astype(BF).reshape(NT, 16, TOK)
     slot = links.reserve(NT)
@@ -229,7 +299,7 @@
     c_in[t] = pj[t]
     for k in range(1, NT):
         links.arrived(slot + k, c_in.at[t_from[k]], dp, t_from[k])
-    summed = res[...].astype(F32)
+    summed = jnp.concatenate([res[...].astype(F32), jnp.zeros((2, TOK), F32)], axis=0)
     for s in range(NT):
         summed = summed + c_in[s].astype(F32)
     summed = summed.astype(BF).astype(F32)
@@ -247,7 +317,6 @@
         links.arrived(slot + k, stream.at[core, y, z_from[k]], group(z_from[k] * 2 + core), t)
     ring_gather(links, stream, dp_of, y, core, t)
 
-    nn = ((1,), (0,))
     slot = links.reserve(NT)
     columns = stream[...].reshape(1024, TOK)
     for k in range(1, NT + 1):
@@ -276,10 +345,9 @@
         links.arrived(slot + k, h_all.at[t_from[k]], dp, t_from[k])
 
     place = jnp.logical_and(iota((16, 896), 1) == dp * 14 + iota((16, 896), 0), iota((16, 896), 0) < 14).astype(BF)
-    tn = ((0,), (0,))
     for block in range(TOK // 128):
         lanes = slice(block * 128, (block + 1) * 128)
-        value = dot(h_all[:, :, lanes].reshape(384, 128), w_down[...], tn)
+        value = dot(h_all[:, :, lanes].reshape(384, 128), w_d[...], tn)
         part[lanes] = value + dot(stream[core, y, z, :, lanes], place, tn)
 
     partner = dp + 1 - 2 * core
@@ -309,7 +377,7 @@
     links.arrived(to_right + 3, r_in.at[3], left, t)
     links.arrived(to_left + 2, l_in.at[2], right, t)
     value = (acc[y] + r_in[3].astype(F32) + l_in[2].astype(F32)).astype(BF)
-    row, col = iota((128, 80), 0), iota((128, 80), 1)
+    row, col = iota((128, 1), 0), iota((128, 80), 1)
     spread = jnp.logical_and(lax.rem(row, 16) < 10, col == (row // 16) * 10 + lax.rem(row, 16)).astype(BF)
     g_out[...] = dot(spread, value, nn).astype(BF).reshape(NG, 16, KVL)
     slot = links.reserve(NG)
@@ -328,11 +396,23 @@
     links.finish()
 
 
-SLOTS = 8 * 7 + 2 * 15 + 4 + 8
+SLOTS = 8 * 11 + 2 * 15 + 4 + 8
 
 
 def layer(*operands):
     scratch = [
+        ((144, LAT), BF),
+        ((NY, 48, 384), BF),
+        ((NY, 48, 384), BF),
+        ((NG, 48, 384), BF),
+        ((NG, 48, 384), BF),
+        ((NG, 48, 192), BF),
+        ((NG, 48, 192), BF),
+        ((NY, 48, 192), BF),
+        ((NY, 48, 192), BF),
+        ((NT * 80, 1024), BF),
+        ((128, 1024), BF),
+        ((384, 896), BF),
         ((NT, REQ, 16, LAT), BF),
         ((REQ, KEYS, LAT), BF),
         ((NT, REQ, 16, 640), BF),
@@ -362,7 +442,7 @@
     return pl.pallas_call(
         kernel,
         out_shape=jax.ShapeDtypeStruct((10, 896), BF),
-        in_specs=[smem] * 2 + [vmem] * 9,
+        in_specs=[smem] * 2 + [vmem] * 12,
         out_specs=vmem,
         scratch_shapes=[pltpu.VMEM(shape, kind) for shape, kind in scratch]
         + [pltpu.SemaphoreType.DMA((SLOTS,)), pltpu.SemaphoreType.DMA((SLOTS,))],
@@ -390,34 +470,22 @@
     w_up,
     w_down,
 ):
-    t = lax.axis_index("tp")
-    own = lax.dynamic_slice(pool, (0, 2 * t, 0), (POOL, 2, LAT)).reshape(2 * POOL, LAT)
-    order = jnp.arange(CAP * 28, dtype=jnp.int32) % CAP
-    row = jnp.arange(512, dtype=jnp.int32)
-    match = jnp.logical_and(
-        mig_dest[0][None, :] == (row // 8)[:, None], order[None, :] == ((row % 8) // 2)[:, None]
+    return layer(
+        page_table,
+        lengths,
+        mig_page,
+        mig_dest,
+        queries.reshape(REQ, 16, LAT),
+        pool.reshape(POOL * PAGE, LAT),
+        new_latent,
+        w_uv,
+        w_out.transpose(2, 1, 0).reshape(112, 1024),
+        residual.reshape(TOK, 14).T,
+        norm_gain.reshape(1, 896),
+        w_gate.T,
+        w_up.T,
+        w_down,
     )
-    source = jnp.sum(jnp.where(match, 2 * mig_page[0][None, :] + 1 + (row % 2)[:, None], 0), axis=1) - 1
-    select = (source[:, None] == jnp.arange(2 * POOL, dtype=jnp.int32)[None, :]).astype(BF)
-    outgoing = jnp.dot(select, own, preferred_element_type=F32).astype(BF).reshape(64, 8, LAT)
-    inbox = lax.all_to_all(outgoing, "dp", split_axis=0, concat_axis=0, tiled=True).reshape(512, LAT)
-
-    gain = norm_gain.astype(F32)[:, None]
-
-    def widen(w):
-        w = (w.astype(F32) * gain).astype(BF).reshape(64, 14, NT, 36)
-        return jnp.pad(w, ((0, 0), (0, 2), (0, 0), (0, 4)))
-
-    w_gu = jnp.stack([widen(w_gate), widen(w_up)], axis=3)
-    inner, slot = jnp.arange(16)[:, None], jnp.arange(80)[None, :]
-    ones = jnp.logical_and(inner >= 14, slot == 36).reshape(1, 16, 1, 2, 40)
-    w_gu = jnp.where(ones, jnp.ones((), BF), w_gu)
-    w_gu = w_gu.reshape(NY, 4, 2, 16, TOK).transpose(4, 2, 0, 1, 3).reshape(TOK, 1024)
-    w_out_t = jnp.pad(w_out, ((0, 0), (0, 0), (0, 2))).reshape(1024, 128).T
-    res_t = jnp.pad(residual.reshape(TOK, 14).T, ((0, 2), (0, 0)))
-    w_down_p = jnp.pad(w_down.reshape(NT, 36, 896), ((0, 0), (0, 12), (0, 0))).reshape(384, 896)
-    q = queries.reshape(REQ, 16, LAT)
-    return layer(page_table, lengths, q, own, inbox, new_latent, w_uv, w_out_t, res_t, w_gu, w_down_p)
 
 
 def solution(mesh):

time: 204 us -> 163 us (0.80)
  local copies, waits for them, and re-layouts: 47.8 us -> 12.9 us
  starting transfers between devices: 17.8 us -> 0 us
  Pallas kernels: 133 us -> 148 us
  other arithmetic: 3.66 us -> 0 us
    another operation x3 -> x0, local copies, waits for them, and re-layouts: 24.3 us -> none  [local(): w_gu = jnp.stack([widen(w_gate), widen(w_up)], axis=3)]
    all_to_all x1 -> x0, starting transfers between devices: 17.8 us -> none  [local(): lax.all_to_all(outgoing, 'dp', split_axis=0, concat_axis=0, tiled=True)]
    pallas_call x1, Pallas kernels: 133 us -> 148 us  [layer(): pl.pallas_call(kernel, out_shape=jax.ShapeDtypeStruct((10, 896), BF), in_...]
    reshape x5 -> x1, local copies, waits for them, and re-layouts: 9.43 us -> 0.69 us  [local(): norm_gain.reshape(1, 896)]
    unnamed x26 -> x27, local copies, waits for them, and re-layouts: 6.08 us -> 12.2 us
    convert_element_type x3 -> x0, local copies, waits for them, and re-layouts: 4.41 us -> none  [the longest x2 3.31 us: widen(): w = (w.astype(F32) * gain).astype(BF).reshape(64, 14, NT, 36)]
  transfers between devices with their start and end apart: 1 -> 0, of which waited for: 0 -> 0; matrix products, arithmetic and copies ran while one was open for 21% -> 0% of each run, Pallas kernels for 0% -> 0%
where the time goes in v2:
time: 163 us; the launch traced here: 161 us
  Pallas kernels  148 us (91%)
  local copies, waits for them, and re-layouts  12.9 us (8%)
    pallas_call x1, Pallas kernels, layer(): pl.pallas_call(kernel, out_shape=jax.ShapeDtypeStruct((10, 896), BF), in_...  148 us
    unnamed x27, local copies, waits for them, and re-layouts  12.2 us

profile of v2, /device:TPU:1, one launch (start us, length us, event | category | flops | bytes accessed | tf_op | source)
XLA Modules:
  0.0 161.3 jit_solution(6059352918535605761)
XLA Ops:
  0.0 0.7 reshape.19.gain
  0.7 0.0 copy-start
  0.7 1.3 copy-done
  2.0 0.0 copy-start.1
  2.0 1.2 copy-done.1
  3.2 0.0 copy-start.2
  3.2 1.0 copy-done.2
  4.3 0.0 copy-start.3
  4.3 1.0 copy-done.3
  5.3 0.0 copy-start.4
  5.3 1.0 copy-done.4
  6.4 0.0 copy-start.5
  6.4 0.9 copy-done.5
  7.3 0.0 copy-start.6
  7.3 0.9 copy-done.6
  8.2 0.0 copy-start.7
  8.2 0.7 copy-done.7
  8.9 0.7 copy-done.8
  9.6 0.7 copy-done.9
  10.3 0.7 copy-done.10
  11.0 0.7 copy-done.11
  11.6 0.7 copy-done.12
  12.3 148.4 %layer.1 = bf16[10,896]{1,0:T(8,128)(2,1)S(1)} custom-call(s32[5,13]{1,0:T(8,128)S(1)} %copy-done.9, s32[5]{0:T(128)S(1)} %copy-done.10, s32[1,84]{1,0:T(1,128)S(1)} %copy-done.11, s32[1,84]{1,0:T(1,128)S(1)} %copy-done.12, bf16[5,16,576]{2,1,0:T(8,128)(2,1)S(1)} %bitcast.14, bf16[1040,576]{1,0:T(8,128)(2,1)S(1)} %bitcast.10, bf16[10,576]{1,0:T(8,128)(2,1)S(1)} %copy-done.7, ...), custom_call_target="tpu_custom_call" | custom-call | flops 3000000000 | bytes 10000000 | tf_op jit(solution)/shard_map/layer/pallas_call | solution.py:442
  160.7 0.6 copy.16
  (5 shorter events, 0.0 us)
Async XLA Ops:
  0.7 1.3 copy-start
  2.0 1.2 copy-start.1
  3.2 1.0 copy-start.2
  4.3 1.0 copy-start.3
  5.3 1.0 copy-start.4
  6.4 0.9 copy-start.5
  7.3 0.9 copy-start.6
  8.2 0.7 copy-start.7
  8.9 0.7 copy-start.8
  9.6 0.7 copy-start.9
  10.3 0.7 copy-start.10
  11.0 0.7 copy-start.11
  11.6 0.7 copy-start.12

commit v3 on v2

--- a/solution.py
+++ b/solution.py
@@ -33,6 +33,14 @@
     return lax.dot_general(a, b, (dims, ((), ())), preferred_element_type=F32)
 
 
+def div(value, by):
+    return lax.shift_right_logical(value * (-(-(1 << 20) // by)), 20)
+
+
+def rem(value, by):
+    return value - by * div(value, by)
+
+
 def iota(shape, axis):
     return lax.broadcasted_iota(jnp.int32, shape, axis)
 
@@ -100,11 +108,21 @@
 
 
 def kernel(
-    table, lengths, mig_page, mig_dest, q, pool, fresh, w_uv, w_out, res, gain, w_gate, w_up, w_down, out,
+    *refs
+):
+    operands, (out, *held), rest = refs[:14], refs[14:29], refs[29:]
+    (
+        table, lengths, mig_page, mig_dest, q, pool, fresh, w_uv, w_out, res, gain, w_gate, w_up, w_down
+    ) = held
+    (
     own, a_y1, a_y2, a_y3, a_y4, a_z1, a_z2, a_z3, a_z4, w_gu, w_o, w_d,
     q_all, keys, o_out, o_in, ho, b_in, heads, pj, c_in, stream, gu, e_in, h_all, part, f_out, f_in,
-    acc, r_out, r_in, l_out, l_in, g_out, g_in, send_sems, recv_sems,
-):
+    acc, r_out, r_in, l_out, l_in, g_out, g_in, send_sems, recv_sems, load_sems,
+    ) = rest
+    loads = [pltpu.make_async_copy(*pair, load_sems.at[i]) for i, pair in enumerate(zip(operands, held))]
+    for i in (5, 2, 3, 4, 8, 13, 10, 11, 12, 6, 0, 1, 7, 9):
+        loads[i].start()
+
     dp, t = lax.axis_index("dp"), lax.axis_index("tp")
     y, g = dp // NG, lax.rem(dp, NG)
     z, core = g // 2, lax.rem(g, 2)
@@ -133,20 +151,22 @@
     for k in range(1, NY):
         pl.semaphore_signal(barrier, inc=1, device_id={"dp": dp_of(y_to[k]), "tp": t}, device_id_type=MESH)
 
+    for i in (5, 2, 3, 4):
+        loads[i].wait()
     row = iota((144, 1), 0)
-    column = (row // 2) * PAGE + 2 * t + lax.rem(row, 2)
+    column = (div(row, 2)) * PAGE + 2 * t + rem(row, 2)
     own[...] = dot((column == iota((144, POOL * PAGE), 1)).astype(BF), pool[...], nn).astype(BF)
     row = iota((384, 1), 0)
-    inner = lax.rem(row, 6)
-    entry = lax.rem(iota((1, CAP * 28), 1), CAP)
+    inner = rem(row, 6)
+    entry = rem(iota((1, CAP * 28), 1), CAP)
 
     def outgoing(rank):
-        match = jnp.logical_and(mig_dest[...] == rank, entry == inner // 2)
+        match = jnp.logical_and(mig_dest[...] == rank, entry == div(inner, 2))
         source = jnp.sum(jnp.where(match, (mig_page[...] + 1).astype(F32), 0.0), axis=1, keepdims=True)
-        source = source.astype(jnp.int32) * 2 - 2 + lax.rem(inner, 2)
+        source = source.astype(jnp.int32) * 2 - 2 + rem(inner, 2)
         return (source == iota((384, 144), 1)).astype(BF)
 
-    first, second = row // 48, lax.rem(row, 48) // 6
+    first, second = div(row, 48), div(rem(row, 48), 6)
     a_y1[...] = dot(outgoing(first * NG + second), own[:, :384], nn).astype(BF).reshape(NY, 48, 384)
     a_z1[...] = dot(outgoing(second * NG + first), own[:, 384:], nn).astype(BF).reshape(NG, 48, 192)
     q_all[t] = q[...]
@@ -162,18 +182,20 @@
     a_y2[y] = a_y1[y]
     a_z2[g] = a_z1[g]
 
+    for i in (8, 13, 10, 11, 12):
+        loads[i].wait()
     row, col = iota((128, 1), 0), iota((128, 112), 1)
-    spread = jnp.logical_and(lax.rem(row, 16) < 14, col == lax.rem(row, 16) * 8 + row // 16).astype(BF)
+    spread = jnp.logical_and(rem(row, 16) < 14, col == rem(row, 16) * 8 + div(row, 16)).astype(BF)
     w_o[...] = dot(spread, w_out[...], nn).astype(BF)
     row, col = iota((384, 1), 0), iota((384, 288), 1)
-    spread = jnp.logical_and(lax.rem(row, 48) < 36, col == (row // 48) * 36 + lax.rem(row, 48)).astype(BF)
+    spread = jnp.logical_and(rem(row, 48) < 36, col == (div(row, 48)) * 36 + rem(row, 48)).astype(BF)
     w_d[...] = dot(spread, w_down[...], nn).astype(BF)
 
     for k in range(1, NY):
         links.arrived(along_y + k, a_y2.at[y_from[k]], dp_of(y_from[k]), t)
         links.arrived(along_g + k, a_z2.at[g_from[k]], group(g_from[k]), t)
     row, col = iota((384, 1), 0), iota((384, 384), 1)
-    swap = (col == (lax.rem(row, 48) // 6) * 48 + (row // 48) * 6 + lax.rem(row, 6)).astype(BF)
+    swap = (col == (div(rem(row, 48), 6)) * 48 + (div(row, 48)) * 6 + rem(row, 6)).astype(BF)
     a_y3[...] = dot(swap, a_y2[...].reshape(384, 384), nn).astype(BF).reshape(NG, 48, 384)
     a_z3[...] = dot(swap, a_z2[...].reshape(384, 192), nn).astype(BF).reshape(NY, 48, 192)
     along_g, along_y = links.reserve(NG), links.reserve(NY)
@@ -184,35 +206,37 @@
     a_z4[y] = a_z3[y]
 
     row, col = iota((NT * 80, 1), 0), iota((NT * 80, 288), 1)
-    slot = lax.rem(row, 80)
-    of_gate = jnp.logical_and(slot < 36, col == (row // 80) * 36 + slot).astype(BF)
-    of_up = jnp.logical_and(jnp.logical_and(slot >= 40, slot < 76), col == (row // 80) * 36 + slot - 40).astype(BF)
+    slot = rem(row, 80)
+    of_gate = jnp.logical_and(slot < 36, col == (div(row, 80)) * 36 + slot).astype(BF)
+    of_up = jnp.logical_and(jnp.logical_and(slot >= 40, slot < 76), col == (div(row, 80)) * 36 + slot - 40).astype(BF)
     scale = gain[...].astype(F32)
     rows = dot(of_gate, (w_gate[...].astype(F32) * scale).astype(BF), nn)
     rows = (rows + dot(of_up, (w_up[...].astype(F32) * scale).astype(BF), nn)).astype(BF)
     row, col = iota((896, 1), 0), iota((896, 1024), 1)
-    rank = row // 14
-    at = lax.rem(rank, 2) * 512 + (rank // 2) * 16 + lax.rem(row, 14)
+    rank = div(row, 14)
+    at = rem(rank, 2) * 512 + (div(rank, 2)) * 16 + rem(row, 14)
     spread = (col == at).astype(BF)
-    squares_at = jnp.logical_and(lax.rem(iota((NT * 80, 1), 0), 80) == 36, lax.rem(iota((1, 1024), 1), 16) >= 14)
+    squares_at = jnp.logical_and(rem(iota((NT * 80, 1), 0), 80) == 36, rem(iota((1, 1024), 1), 16) >= 14)
     w_gu[...] = jnp.where(squares_at, 1.0, dot(rows, spread, nn)).astype(BF)
 
     for k in range(1, NY):
         links.arrived(along_g + k, a_y4.at[g_from[k]], group(g_from[k]), t)
         links.arrived(along_y + k, a_z4.at[y_from[k]], dp_of(y_from[k]), t)
 
+    for i in (6, 0, 1):
+        loads[i].wait()
     row = iota((REQ * KEYS, 1), 0)
-    place, request = lax.rem(row, KEYS), row // KEYS
+    place, request = rem(row, KEYS), div(row, KEYS)
     named = jnp.full((REQ * KEYS, 1), -1, jnp.int32)
     for r in range(REQ):
         for k in range(MAXP):
-            named = jnp.where(jnp.logical_and(request == r, place // 2 == k), table[r, k], named)
-    token = lax.rem(place, 2)
+            named = jnp.where(jnp.logical_and(request == r, div(place, 2) == k), table[r, k], named)
+    token = rem(place, 2)
     from_own = (jnp.where(jnp.logical_and(named >= 0, named < POOL), 2 * named + token, -1) == iota((REQ * KEYS, 144), 1)).astype(BF)
     migrated = jnp.maximum(named - POOL, 0)
-    rank = (migrated * 171) // 512
+    rank = div(migrated, 3)
     inner = (migrated - CAP * rank) * 2 + token
-    rank_y, rank_g = rank // NG, lax.rem(rank, NG)
+    rank_y, rank_g = div(rank, NG), rem(rank, NG)
     in_inbox = named >= POOL
     at = jnp.where(in_inbox, rank_g * 48 + rank_y * 6 + inner, -1)
     from_y = (at == iota((REQ * KEYS, 384), 1)).astype(BF)
@@ -235,8 +259,8 @@
     length = jnp.full((REQ * 128, 1), lengths[0], jnp.int32)
     for r in range(1, REQ):
         length = jnp.where(row >= r * 128, lengths[r], length)
-    cached = jnp.logical_and(col < 26, (col // 2) * PAGE + 2 * t + lax.rem(col, 2) < length)
-    newer = jnp.logical_and(jnp.logical_and(col >= 26, col <= 26 + lax.rem(row // 8, 2)), t == 0)
+    cached = jnp.logical_and(col < 26, (div(col, 2)) * PAGE + 2 * t + rem(col, 2) < length)
+    newer = jnp.logical_and(jnp.logical_and(col >= 26, col <= 26 + rem(div(row, 8), 2)), t == 0)
     live = jnp.logical_or(cached, newer)
     scores = jnp.where(live, scores, DEAD)
     top = jnp.max(scores, axis=1, keepdims=True)
@@ -270,8 +294,10 @@
         latent = latent + o_in[s, :, :, :KVL].astype(F32) * (shares[s] / total)
     latent = latent.astype(BF).reshape(REQ * 16, KVL)
 
-    of_token = (iota((16, 80), 1) // 8 == iota((16, 80), 0)).astype(BF)
-    head = lax.rem(iota((80, HD), 0), 8)
+    for i in (7, 9):
+        loads[i].wait()
+    of_token = (div(iota((16, 80), 1), 8) == iota((16, 80), 0)).astype(BF)
+    head = rem(iota((80, HD), 0), 8)
     for h in range(8):
         values = jnp.where(head == h, dot(latent, w_uv[h], ((1,), (0,))), 0.0).astype(BF)
         values = dot(of_token, values, ((1,), (0,))).astype(BF)
@@ -284,7 +310,7 @@
     for k in range(1, NG):
         links.arrived(slot + k, b_in.at[g_from[k]], group(g_from[k]), t)
     row, col = iota((80, 1), 0), iota((80, 128), 1)
-    pack = (col == (row // 10) * 16 + lax.rem(row, 10)).astype(BF)
+    pack = (col == (div(row, 10)) * 16 + rem(row, 10)).astype(BF)
     heads[core, y] = dot(pack, b_in[...].reshape(128, KVL), ((1,), (0,))).astype(BF)
     ring_gather(links, heads, dp_of, y, core, t)
 
@@ -378,7 +404,7 @@
     links.arrived(to_left + 2, l_in.at[2], right, t)
     value = (acc[y] + r_in[3].astype(F32) + l_in[2].astype(F32)).astype(BF)
     row, col = iota((128, 1), 0), iota((128, 80), 1)
-    spread = jnp.logical_and(lax.rem(row, 16) < 10, col == (row // 16) * 10 + lax.rem(row, 16)).astype(BF)
+    spread = jnp.logical_and(rem(row, 16) < 10, col == (div(row, 16)) * 10 + rem(row, 16)).astype(BF)
     g_out[...] = dot(spread, value, nn).astype(BF).reshape(NG, 16, KVL)
     slot = links.reserve(NG)
     for k in range(1, NG):
@@ -437,17 +463,20 @@
         ((NG, 16, KVL), BF),
         ((NG, 16, KVL), BF),
     ]
-    smem = pl.BlockSpec(memory_space=pltpu.SMEM)
     vmem = pl.BlockSpec(memory_space=pltpu.VMEM)
+    held = [
+        (pltpu.SMEM if i < 2 else pltpu.VMEM)(operand.shape, operand.dtype) for i, operand in enumerate(operands)
+    ]
     return pl.pallas_call(
         kernel,
         out_shape=jax.ShapeDtypeStruct((10, 896), BF),
-        in_specs=[smem] * 2 + [vmem] * 12,
+        in_specs=[pl.BlockSpec(memory_space=pl.ANY)] * 14,
         out_specs=vmem,
-        scratch_shapes=[pltpu.VMEM(shape, kind) for shape, kind in scratch]
-        + [pltpu.SemaphoreType.DMA((SLOTS,)), pltpu.SemaphoreType.DMA((SLOTS,))],
+        scratch_shapes=held
+        + [pltpu.VMEM(shape, kind) for shape, kind in scratch]
+        + [pltpu.SemaphoreType.DMA((SLOTS,)), pltpu.SemaphoreType.DMA((SLOTS,)), pltpu.SemaphoreType.DMA((14,))],
         compiler_params=pltpu.CompilerParams(
-            collective_id=0, has_side_effects=True, vmem_limit_bytes=48 * 1024 * 1024
+            collective_id=0, has_side_effects=True, vmem_limit_bytes=60 * 1024 * 1024
         ),
         cost_estimate=pl.CostEstimate(flops=3 * 10**9, bytes_accessed=10**7, transcendentals=10**6),
         name="layer",

time: 163 us -> 154 us (0.945)
  local copies, waits for them, and re-layouts: 12.9 us -> 2.62 us
  Pallas kernels: 148 us -> 151 us
    unnamed x27 -> x1, local copies, waits for them, and re-layouts: 12.2 us -> 1.36 us
    pallas_call x1, Pallas kernels: 148 us -> 151 us  [layer(): pl.pallas_call(kernel, out_shape=jax.ShapeDtypeStruct((10, 896), BF), in_...]
where the time goes in v3:
time: 154 us
  Pallas kernels  151 us (98%)
  local copies, waits for them, and re-layouts  2.62 us (2%)
    pallas_call x1, Pallas kernels, layer(): pl.pallas_call(kernel, out_shape=jax.ShapeDtypeStruct((10, 896), BF), in_...  151 us

profile of v3, /device:TPU:1, one launch (start us, length us, event | category | flops | bytes accessed | tf_op | source)
XLA Modules:
  0.0 153.8 jit_solution(13590206515039521321)
XLA Ops:
  0.0 1.3 reshape.19.refs_10_
  1.3 151.2 %layer.1 = bf16[10,896]{1,0:T(8,128)(2,1)} custom-call(s32[5,13]{1,0:T(8,128)} %refs_0_.1, s32[5]{0:T(128)} %refs_1_.1, s32[1,84]{1,0:T(1,128)} %refs_2_.1, s32[1,84]{1,0:T(1,128)} %refs_3_.1, bf16[5,16,576]{2,1,0:T(8,128)(2,1)} %bitcast.14, bf16[1040,576]{1,0:T(8,128)(2,1)} %bitcast.10, bf16[10,576]{1,0:T(8,128)(2,1)} %refs_6_.1, ...), custom_call_target="tpu_custom_call" | custom-call | flops 3000000000 | bytes 10000000 | tf_op jit(solution)/shard_map/layer/pallas_call | solution.py:470
  152.5 1.4 copy.16

commit v4 on v3

--- a/solution.py
+++ b/solution.py
@@ -27,6 +27,9 @@
 F32 = jnp.float32
 MESH = pl.DeviceIdType.MESH
 DEAD = -1e30
+ROWS = (48, 32)
+PER_HALF = 14
+DONE = object()
 
 
 def dot(a, b, dims):
@@ -77,36 +80,6 @@
             copy.wait_send()
 
 
-def ring_gather(links, buf, dp_of, y, core, tp):
-    right, left = dp_of(lax.rem(y + 1, NY)), dp_of(lax.rem(y + NY - 1, NY))
-    partner = dp_of(y) + 1 - 2 * core
-    to_right, to_left, over = links.reserve(4), links.reserve(3), links.reserve(8)
-
-    def pass_on(order, index):
-        links.send(over + order, buf.at[core, index], buf.at[core, index], partner, tp)
-
-    links.send(to_right, buf.at[core, y], buf.at[core, y], right, tp)
-    links.send(to_left, buf.at[core, y], buf.at[core, y], left, tp)
-    pass_on(0, y)
-    indices = [y]
-    for step in range(4):
-        index = lax.rem(y + NY - 1 - step, NY)
-        links.arrived(to_right + step, buf.at[core, index], left, tp)
-        if step < 3:
-            links.send(to_right + step + 1, buf.at[core, index], buf.at[core, index], right, tp)
-        pass_on(len(indices), index)
-        indices.append(index)
-        if step < 3:
-            index = lax.rem(y + 1 + step, NY)
-            links.arrived(to_left + step, buf.at[core, index], right, tp)
-            if step < 2:
-                links.send(to_left + step + 1, buf.at[core, index], buf.at[core, index], left, tp)
-            pass_on(len(indices), index)
-            indices.append(index)
-    for order, index in enumerate(indices):
-        links.arrived(over + order, buf.at[1 - core, index], partner, tp)
-
-
 def kernel(
     *refs
 ):
@@ -116,11 +89,10 @@
     ) = held
     (
     own, a_y1, a_y2, a_y3, a_y4, a_z1, a_z2, a_z3, a_z4, w_gu, w_o, w_d,
-    q_all, keys, o_out, o_in, ho, b_in, heads, pj, c_in, stream, gu, e_in, h_all, part, f_out, f_in,
-    acc, r_out, r_in, l_out, l_in, g_out, g_in, send_sems, recv_sems, load_sems,
+    q_all, keys, o_out, o_in, ho, b_in, last, g_out, g_in, *halves, send_sems, recv_sems, load_sems,
     ) = rest
     loads = [pltpu.make_async_copy(*pair, load_sems.at[i]) for i, pair in enumerate(zip(operands, held))]
-    for i in (5, 2, 3, 4, 8, 13, 10, 11, 12, 6, 0, 1, 7, 9):
+    for i in (5, 2, 3, 4, 8, 9, 13, 10, 11, 12, 6, 0, 1, 7):
         loads[i].start()
 
     dp, t = lax.axis_index("dp"), lax.axis_index("tp")
@@ -182,7 +154,7 @@
     a_y2[y] = a_y1[y]
     a_z2[g] = a_z1[g]
 
-    for i in (8, 13, 10, 11, 12):
+    for i in (8, 9, 13, 10, 11, 12):
         loads[i].wait()
     row, col = iota((128, 1), 0), iota((128, 112), 1)
     spread = jnp.logical_and(rem(row, 16) < 14, col == rem(row, 16) * 8 + div(row, 16)).astype(BF)
@@ -190,6 +162,11 @@
     row, col = iota((384, 1), 0), iota((384, 288), 1)
     spread = jnp.logical_and(rem(row, 48) < 36, col == (div(row, 48)) * 36 + rem(row, 48)).astype(BF)
     w_d[...] = dot(spread, w_down[...], nn).astype(BF)
+    for h, rows in enumerate(ROWS):
+        row, col = iota((TOK, 1), 0), iota((1, NY * rows), 1)
+        at = div(col, rows) * 80 + rem(col, rows) + h * ROWS[0]
+        values = dot(res[...], (row == at).astype(BF), nn)
+        halves[h * PER_HALF][...] = jnp.concatenate([values, jnp.zeros((2, NY * rows), F32)], axis=0)
 
     for k in range(1, NY):
         links.arrived(along_y + k, a_y2.at[y_from[k]], dp_of(y_from[k]), t)
@@ -294,7 +271,7 @@
         latent = latent + o_in[s, :, :, :KVL].astype(F32) * (shares[s] / total)
     latent = latent.astype(BF).reshape(REQ * 16, KVL)
 
-    for i in (7, 9):
+    for i in (7,):
         loads[i].wait()
     of_token = (div(iota((16, 80), 1), 8) == iota((16, 80), 0)).astype(BF)
     head = rem(iota((80, HD), 0), 8)
@@ -309,103 +286,174 @@
     b_in[g] = ho[core]
     for k in range(1, NG):
         links.arrived(slot + k, b_in.at[g_from[k]], group(g_from[k]), t)
-    row, col = iota((80, 1), 0), iota((80, 128), 1)
-    pack = (col == (div(row, 10)) * 16 + rem(row, 10)).astype(BF)
-    heads[core, y] = dot(pack, b_in[...].reshape(128, KVL), ((1,), (0,))).astype(BF)
-    ring_gather(links, heads, dp_of, y, core, t)
-
-    for half in range(2):
-        x = heads[half].reshape(TOK, KVL)
-        add = dot(w_o[:, half * KVL : (half + 1) * KVL], x, nt)
-        projected = add if half == 0 else projected + add
-    pj[...] = projected.astype(BF).reshape(NT, 16, TOK)
-    slot = links.reserve(NT)
-    for k in range(1, NT):
-        links.send(slot + k, pj.at[t_to[k]], c_in.at[t], dp, t_to[k])
-    c_in[t] = pj[t]
-    for k in range(1, NT):
-        links.arrived(slot + k, c_in.at[t_from[k]], dp, t_from[k])
-    summed = jnp.concatenate([res[...].astype(F32), jnp.zeros((2, TOK), F32)], axis=0)
-    for s in range(NT):
-        summed = summed + c_in[s].astype(F32)
-    summed = summed.astype(BF).astype(F32)
-    squares = jnp.sum(summed * summed, axis=0, keepdims=True)
-    high = squares.astype(BF).astype(F32)
-    row = iota((16, TOK), 0)
-    piece = jnp.where(row == 14, high, jnp.where(row == 15, squares - high, summed)).astype(BF)
-    stream[core, y, z] = piece
-
-    slot = links.reserve(4)
-    for k in range(1, 4):
-        mine = stream.at[core, y, z]
-        links.send(slot + k, mine, mine, group(z_to[k] * 2 + core), t)
-    for k in range(1, 4):
-        links.arrived(slot + k, stream.at[core, y, z_from[k]], group(z_from[k] * 2 + core), t)
-    ring_gather(links, stream, dp_of, y, core, t)
-
-    slot = links.reserve(NT)
-    columns = stream[...].reshape(1024, TOK)
-    for k in range(1, NT + 1):
-        to = lax.rem(t + k, NT)
-        first = pl.multiple_of(to * 80, 80)
-        gu[to] = dot(w_gu[pl.ds(first, 80), :], columns, nn).astype(BF)
-        if k < NT:
-            links.send(slot + k, gu.at[to], e_in.at[t], dp, to)
+    partner = dp + 1 - 2 * core
+
+    def at_y(step):
+        return lax.rem(y + NY + step, NY)
+
+    def gather(buf, flip):
+        near, far, over = links.reserve(4), links.reserve(3), links.reserve(8)
+        held_y = []
+
+        def pass_on(index):
+            links.send(over + len(held_y), buf.at[core, index], buf.at[core, index], partner, t)
+            held_y.append(index)
+
+        def forward(slot, index, step):
+            links.send(slot, buf.at[core, index], buf.at[core, index], dp_of(at_y(step)), t)
+
+        def arrived(slot, index):
+            links.arrived(slot, buf.at[core, index], partner, t)
+
+        for i, step in enumerate((2, -2, 1, -1)):
+            forward(near + i, y, step)
+        pass_on(y)
+        yield
+        arrived(near, at_y(-2))
+        forward(far, at_y(-2), 1)
+        if flip:
+            forward(far + 2, at_y(-2), 2)
+        arrived(near + 1, at_y(2))
+        forward(far + 1, at_y(2), -1)
+        if not flip:
+            forward(far + 2, at_y(2), -2)
+        pass_on(at_y(-2))
+        pass_on(at_y(2))
+        for i, step in ((2, -1), (3, 1)):
+            arrived(near + i, at_y(step))
+            pass_on(at_y(step))
+        yield
+        for i, step in ((0, -3), (1, 3), (2, 4)):
+            arrived(far + i, at_y(step))
+            pass_on(at_y(step))
+        for order, index in enumerate(held_y):
+            links.arrived(over + order, buf.at[1 - core, index], partner, t)
+
+    def scatter(acc, r_out, r_in, flip):
+        slot = links.reserve(7)
+
+        def send(i, value, step):
+            r_out[i] = value.astype(BF)
+            links.send(slot + i, r_out.at[i], r_in.at[i], dp_of(at_y(step)), t)
+
+        def received(i):
+            links.arrived(slot + i, r_in.at[i], partner, t)
+            return r_in[i].astype(F32)
+
+        send(2, acc[at_y(4)], 2 if flip else -2)
+        send(0, acc[at_y(-3)], -1)
+        send(1, acc[at_y(3)], 1)
+        send(3, acc[at_y(-1)], -1)
+        send(4, acc[at_y(1)], 1)
+        yield
+        below, above = acc[at_y(-2)] + received(0), acc[at_y(2)] + received(1)
+        if flip:
+            above = above + received(2)
         else:
-            e_in[t] = gu[t]
-    for k in range(1, NT):
-        links.arrived(slot + k, e_in.at[t_from[k]], dp, t_from[k])
-    total = jnp.zeros((80, TOK), F32)
-    for s in range(NT):
-        total = total + e_in[s].astype(F32)
-    scale = lax.rsqrt(total[36:37] / D + EPS)
-    gate, up = total[:40] * scale, total[40:] * scale
-    hidden = gate / (1.0 + jnp.exp(-gate)) * up
-    hidden = jnp.where(iota((40, TOK), 0) < 36, hidden, 0.0)
-    hidden = jnp.concatenate([hidden, jnp.zeros((8, TOK), F32)], axis=0).astype(BF)
-    h_all[t] = hidden
-    slot = links.reserve(NT)
-    for k in range(1, NT):
-        links.send(slot + k, h_all.at[t], h_all.at[t], dp, t_to[k])
-    for k in range(1, NT):
-        links.arrived(slot + k, h_all.at[t_from[k]], dp, t_from[k])
+            below = below + received(2)
+        send(5, below, -2)
+        send(6, above, 2)
+        yield
+        value = acc[y]
+        for i in range(3, 7):
+            value = value + received(i)
+        return value
+
+    def chain(h):
+        rows = ROWS[h]
+        lanes = NY * rows
+        (
+            res_h, heads, pj, c_in, stream, gu, e_in, h_all, part, f_out, f_in, acc, r_out, r_in
+        ) = halves[h * PER_HALF : (h + 1) * PER_HALF]
+        yield from gather(heads, h)
+
+        projected = dot(w_o[:, :KVL], heads[0].reshape(lanes, KVL), nt)
+        projected = projected + dot(w_o[:, KVL:], heads[1].reshape(lanes, KVL), nt)
+        pj[...] = projected.astype(BF).reshape(NT, 16, lanes)
+        slot = links.reserve(NT)
+        for k in range(1, NT):
+            links.send(slot + k, pj.at[t_to[k]], c_in.at[t], dp, t_to[k])
+        c_in[t] = pj[t]
+        yield
+        for k in range(1, NT):
+            links.arrived(slot + k, c_in.at[t_from[k]], dp, t_from[k])
+        summed = res_h[...]
+        for s in range(NT):
+            summed = summed + c_in[s].astype(F32)
+        summed = summed.astype(BF).astype(F32)
+        squares = jnp.sum(summed * summed, axis=0, keepdims=True)
+        high = squares.astype(BF).astype(F32)
+        row = iota((16, lanes), 0)
+        piece = jnp.where(row == 14, high, jnp.where(row == 15, squares - high, summed)).astype(BF)
+        stream[core, y, z] = piece
+
+        slot = links.reserve(4)
+        for k in range(1, 4):
+            block = stream.at[core, y, z]
+            links.send(slot + k, block, block, group(z_to[k] * 2 + core), t)
+        yield
+        for k in range(1, 4):
+            links.arrived(slot + k, stream.at[core, y, z_from[k]], group(z_from[k] * 2 + core), t)
+        yield from gather(stream, h)
+
+        slot = links.reserve(NT)
+        columns = stream[...].reshape(1024, lanes)
+        for k in range(1, NT + 1):
+            to = lax.rem(t + k, NT)
+            first = pl.multiple_of(to * 80, 80)
+            gu[to] = dot(w_gu[pl.ds(first, 80), :], columns, nn).astype(BF)
+            if k < NT:
+                links.send(slot + k, gu.at[to], e_in.at[t], dp, to)
+            else:
+                e_in[t] = gu[t]
+        yield
+        for k in range(1, NT):
+            links.arrived(slot + k, e_in.at[t_from[k]], dp, t_from[k])
+        total = jnp.zeros((80, lanes), F32)
+        for s in range(NT):
+            total = total + e_in[s].astype(F32)
+        scale = lax.rsqrt(total[36:37] / D + EPS)
+        gate, up = total[:40] * scale, total[40:] * scale
+        hidden = gate / (1.0 + jnp.exp(-gate)) * up
+        hidden = jnp.where(iota((40, lanes), 0) < 36, hidden, 0.0)
+        hidden = jnp.concatenate([hidden, jnp.zeros((8, lanes), F32)], axis=0).astype(BF)
+        h_all[t] = hidden
+        slot = links.reserve(NT)
+        for k in range(1, NT):
+            links.send(slot + k, h_all.at[t], h_all.at[t], dp, t_to[k])
+        yield
+        for k in range(1, NT):
+            links.arrived(slot + k, h_all.at[t_from[k]], dp, t_from[k])
+
+        for block in range(lanes // 128):
+            span = slice(block * 128, (block + 1) * 128)
+            value = dot(h_all[:, :, span].reshape(384, 128), w_d[...], tn)
+            part[span] = value + dot(stream[core, y, z, :, span], place, tn)
+
+        f_out[...] = part[:, other].astype(BF)
+        slot = links.reserve(1)
+        links.send(slot, f_out, f_in, partner, t)
+        yield
+        links.arrived(slot, f_in, partner, t)
+        acc[...] = (part[:, mine] + f_in[...].astype(F32)).reshape(NY, rows, KVL)
+        value = yield from scatter(acc, r_out, r_in, h)
+        last[h * ROWS[0] : h * ROWS[0] + rows] = value.astype(BF)
 
     place = jnp.logical_and(iota((16, 896), 1) == dp * 14 + iota((16, 896), 0), iota((16, 896), 0) < 14).astype(BF)
-    for block in range(TOK // 128):
-        lanes = slice(block * 128, (block + 1) * 128)
-        value = dot(h_all[:, :, lanes].reshape(384, 128), w_d[...], tn)
-        part[lanes] = value + dot(stream[core, y, z, :, lanes], place, tn)
-
-    partner = dp + 1 - 2 * core
     mine = pl.ds(pl.multiple_of(core * 384, 128), KVL)
     other = pl.ds(pl.multiple_of((1 - core) * 384, 128), KVL)
-    f_out[...] = part[:, other].astype(BF)
-    slot = links.reserve(1)
-    links.send(slot, f_out, f_in, partner, t)
-    links.arrived(slot, f_in, partner, t)
-    acc[...] = (part[:, mine] + f_in[...].astype(F32)).reshape(NY, 80, KVL)
-    right, left = dp_of(lax.rem(y + 1, NY)), dp_of(lax.rem(y + NY - 1, NY))
-    to_right, to_left = links.reserve(4), links.reserve(3)
-    for step in range(4):
-        value = acc[lax.rem(y + 4 - step, NY)]
-        if step > 0:
-            links.arrived(to_right + step - 1, r_in.at[step - 1], left, t)
-            value = value + r_in[step - 1].astype(F32)
-        r_out[step] = value.astype(BF)
-        links.send(to_right + step, r_out.at[step], r_in.at[step], right, t)
-        if step < 3:
-            value = acc[lax.rem(y + NY - 3 + step, NY)]
-            if step > 0:
-                links.arrived(to_left + step - 1, l_in.at[step - 1], right, t)
-                value = value + l_in[step - 1].astype(F32)
-            l_out[step] = value.astype(BF)
-            links.send(to_left + step, l_out.at[step], l_in.at[step], left, t)
-    links.arrived(to_right + 3, r_in.at[3], left, t)
-    links.arrived(to_left + 2, l_in.at[2], right, t)
-    value = (acc[y] + r_in[3].astype(F32) + l_in[2].astype(F32)).astype(BF)
+    gathered = b_in[...].reshape(128, KVL)
+    for h, rows in enumerate(ROWS):
+        row, col = iota((rows, 1), 0) + h * ROWS[0], iota((rows, 128), 1)
+        pack = (col == div(row, 10) * 16 + rem(row, 10)).astype(BF)
+        halves[h * PER_HALF + 1][core, y] = dot(pack, gathered, nn).astype(BF)
+    running = [chain(h) for h in range(len(ROWS))]
+    while running:
+        running = [steps for steps in running if next(steps, DONE) is not DONE]
+
     row, col = iota((128, 1), 0), iota((128, 80), 1)
     spread = jnp.logical_and(rem(row, 16) < 10, col == (div(row, 16)) * 10 + rem(row, 16)).astype(BF)
-    g_out[...] = dot(spread, value, nn).astype(BF).reshape(NG, 16, KVL)
+    g_out[...] = dot(spread, last[...], nn).astype(BF).reshape(NG, 16, KVL)
     slot = links.reserve(NG)
     for k in range(1, NG):
         links.send(slot + k, g_out.at[g_to[k]], g_in.at[g], group(g_to[k]), t)
@@ -422,7 +470,7 @@
     links.finish()
 
 
-SLOTS = 8 * 11 + 2 * 15 + 4 + 8
+SLOTS = 8 * 8 + 2 * (2 * 15 + 3 * 8 + 4 + 1 + 7)
 
 
 def layer(*operands):
@@ -445,24 +493,28 @@
         ((NT, REQ, 16, 640), BF),
         ((2, 16, KVL), BF),
         ((NG, 16, KVL), BF),
-        ((2, NY, 80, KVL), BF),
-        ((NT, 16, TOK), BF),
-        ((NT, 16, TOK), BF),
-        ((2, NY, 4, 16, TOK), BF),
-        ((NT, 80, TOK), BF),
-        ((NT, 80, TOK), BF),
-        ((NT, 48, TOK), BF),
-        ((TOK, 896), F32),
-        ((TOK, KVL), BF),
-        ((TOK, KVL), BF),
-        ((NY, 80, KVL), F32),
-        ((4, 80, KVL), BF),
-        ((4, 80, KVL), BF),
-        ((3, 80, KVL), BF),
-        ((3, 80, KVL), BF),
+        ((80, KVL), BF),
         ((NG, 16, KVL), BF),
         ((NG, 16, KVL), BF),
     ]
+    for rows in ROWS:
+        lanes = NY * rows
+        scratch += [
+            ((16, lanes), F32),
+            ((2, NY, rows, KVL), BF),
+            ((NT, 16, lanes), BF),
+            ((NT, 16, lanes), BF),
+            ((2, NY, 4, 16, lanes), BF),
+            ((NT, 80, lanes), BF),
+            ((NT, 80, lanes), BF),
+            ((NT, 48, lanes), BF),
+            ((lanes, 896), F32),
+            ((lanes, KVL), BF),
+            ((lanes, KVL), BF),
+            ((NY, rows, KVL), F32),
+            ((7, rows, KVL), BF),
+            ((7, rows, KVL), BF),
+        ]
     vmem = pl.BlockSpec(memory_space=pltpu.VMEM)
     held = [
         (pltpu.SMEM if i < 2 else pltpu.VMEM)(operand.shape, operand.dtype) for i, operand in enumerate(operands)

time: 154 us -> 136 us (0.88)
  Pallas kernels: 151 us -> 133 us
    pallas_call x1, Pallas kernels: 151 us -> 133 us  [layer(): pl.pallas_call(kernel, out_shape=jax.ShapeDtypeStruct((10, 896), BF), in_...]
where the time goes in v4:
time: 136 us
  Pallas kernels  133 us (98%)
  local copies, waits for them, and re-layouts  2.62 us (2%)
    pallas_call x1, Pallas kernels, layer(): pl.pallas_call(kernel, out_shape=jax.ShapeDtypeStruct((10, 896), BF), in_...  133 us

profile of v4, /device:TPU:1, one launch (start us, length us, event | category | flops | bytes accessed | tf_op | source)
XLA Modules:
  0.0 135.8 jit_solution(15142684055424336254)
XLA Ops:
  0.0 1.3 reshape.19.refs_10_
  1.3 133.2 %layer.1 = bf16[10,896]{1,0:T(8,128)(2,1)} custom-call(s32[5,13]{1,0:T(8,128)} %refs_0_.1, s32[5]{0:T(128)} %refs_1_.1, s32[1,84]{1,0:T(1,128)} %refs_2_.1, s32[1,84]{1,0:T(1,128)} %refs_3_.1, bf16[5,16,576]{2,1,0:T(8,128)(2,1)} %bitcast.14, bf16[1040,576]{1,0:T(8,128)(2,1)} %bitcast.10, bf16[10,576]{1,0:T(8,128)(2,1)} %refs_6_.1, ...), custom_call_target="tpu_custom_call" | custom-call | flops 3000000000 | bytes 10000000 | tf_op jit(solution)/shard_map/layer/pallas_call | solution.py:522
  134.4 1.4 %copy.16 = bf16[10,896]{1,0:T(8,128)(2,1)} copy(bf16[10,896]{1,0:T(8,128)(2,1)} %layer.1) | data formatting | bytes 35840

commit v5 on v4

--- a/solution.py
+++ b/solution.py
@@ -27,8 +27,10 @@
 F32 = jnp.float32
 MESH = pl.DeviceIdType.MESH
 DEAD = -1e30
-ROWS = (48, 32)
-PER_HALF = 14
+PARTS = (2, 3)
+FIRST = tuple(sum(PARTS[:h]) for h in range(len(PARTS)))
+PER_PART = 18
+HALF_ROWS = tuple(-(-8 * requests // 16) * 16 for requests in PARTS)
 DONE = object()
 
 
@@ -89,7 +91,7 @@
     ) = held
     (
     own, a_y1, a_y2, a_y3, a_y4, a_z1, a_z2, a_z3, a_z4, w_gu, w_o, w_d,
-    q_all, keys, o_out, o_in, ho, b_in, last, g_out, g_in, *halves, send_sems, recv_sems, load_sems,
+    q_all, keys, last, g_out, g_in, *buffers, send_sems, recv_sems, load_sems,
     ) = rest
     loads = [pltpu.make_async_copy(*pair, load_sems.at[i]) for i, pair in enumerate(zip(operands, held))]
     for i in (5, 2, 3, 4, 8, 9, 13, 10, 11, 12, 6, 0, 1, 7):
@@ -162,11 +164,12 @@
     row, col = iota((384, 1), 0), iota((384, 288), 1)
     spread = jnp.logical_and(rem(row, 48) < 36, col == (div(row, 48)) * 36 + rem(row, 48)).astype(BF)
     w_d[...] = dot(spread, w_down[...], nn).astype(BF)
-    for h, rows in enumerate(ROWS):
-        row, col = iota((TOK, 1), 0), iota((1, NY * rows), 1)
-        at = div(col, rows) * 80 + rem(col, rows) + h * ROWS[0]
+    for h, requests in enumerate(PARTS):
+        tokens = 2 * requests
+        row, col = iota((TOK, 1), 0), iota((1, 64 * tokens), 1)
+        at = div(col, tokens) * 10 + rem(col, tokens) + 2 * FIRST[h]
         values = dot(res[...], (row == at).astype(BF), nn)
-        halves[h * PER_HALF][...] = jnp.concatenate([values, jnp.zeros((2, NY * rows), F32)], axis=0)
+        buffers[h * PER_PART][...] = jnp.concatenate([values, jnp.zeros((2, 64 * tokens), F32)], axis=0)
 
     for k in range(1, NY):
         links.arrived(along_y + k, a_y2.at[y_from[k]], dp_of(y_from[k]), t)
@@ -186,7 +189,7 @@
     slot = rem(row, 80)
     of_gate = jnp.logical_and(slot < 36, col == (div(row, 80)) * 36 + slot).astype(BF)
     of_up = jnp.logical_and(jnp.logical_and(slot >= 40, slot < 76), col == (div(row, 80)) * 36 + slot - 40).astype(BF)
-    scale = gain[...].astype(F32)
+    scale = gain[...].astype(F32).reshape(1, 896)
     rows = dot(of_gate, (w_gate[...].astype(F32) * scale).astype(BF), nn)
     rows = (rows + dot(of_up, (w_up[...].astype(F32) * scale).astype(BF), nn)).astype(BF)
     row, col = iota((896, 1), 0), iota((896, 1024), 1)
@@ -252,40 +255,7 @@
     low = lse - high - middle
     lane = iota((REQ * 128, 128), 1)
     parts = jnp.where(lane == 0, high, jnp.where(lane == 1, middle, jnp.where(lane == 2, low, 0.0))).astype(BF)
-    for r in range(REQ):
-        latent = dot(weights[r * 128 : (r + 1) * 128], keys[r][:, :KVL], nn)
-        o_out[:, r, :, :KVL] = latent.astype(BF).reshape(NT, 16, KVL)
-        o_out[:, r, :, KVL:] = parts[r * 128 : (r + 1) * 128].reshape(NT, 16, 128)
-    slot = links.reserve(NT)
-    for k in range(1, NT):
-        links.send(slot + k, o_out.at[t_to[k]], o_in.at[t], dp, t_to[k])
-    o_in[t] = o_out[t]
-    for k in range(1, NT):
-        links.arrived(slot + k, o_in.at[t_from[k]], dp, t_from[k])
-    lse = [jnp.sum(o_in[s, :, :, KVL:].astype(F32), axis=2, keepdims=True) for s in range(NT)]
-    top = functools.reduce(jnp.maximum, lse)
-    shares = [jnp.exp(v - top) for v in lse]
-    total = functools.reduce(jnp.add, shares)
-    latent = jnp.zeros((REQ, 16, KVL), F32)
-    for s in range(NT):
-        latent = latent + o_in[s, :, :, :KVL].astype(F32) * (shares[s] / total)
-    latent = latent.astype(BF).reshape(REQ * 16, KVL)
-
-    for i in (7,):
-        loads[i].wait()
-    of_token = (div(iota((16, 80), 1), 8) == iota((16, 80), 0)).astype(BF)
-    head = rem(iota((80, HD), 0), 8)
-    for h in range(8):
-        values = jnp.where(head == h, dot(latent, w_uv[h], ((1,), (0,))), 0.0).astype(BF)
-        values = dot(of_token, values, ((1,), (0,))).astype(BF)
-        ho[h // 4, :, (h % 4) * HD : (h % 4 + 1) * HD] = values
-
-    slot = links.reserve(NG)
-    for k in range(1, NG):
-        links.send(slot + k, ho.at[lax.rem(g_to[k], 2)], b_in.at[g], group(g_to[k]), t)
-    b_in[g] = ho[core]
-    for k in range(1, NG):
-        links.arrived(slot + k, b_in.at[g_from[k]], group(g_from[k]), t)
+    loads[7].wait()
     partner = dp + 1 - 2 * core
 
     def at_y(step):
@@ -360,11 +330,56 @@
         return value
 
     def chain(h):
-        rows = ROWS[h]
-        lanes = NY * rows
+        requests = PARTS[h]
+        tokens = 2 * requests
+        rows, lanes = NG * tokens, 64 * tokens
+        padded = HALF_ROWS[h]
         (
-            res_h, heads, pj, c_in, stream, gu, e_in, h_all, part, f_out, f_in, acc, r_out, r_in
-        ) = halves[h * PER_HALF : (h + 1) * PER_HALF]
+            res_h, o_out, o_in, ho, b_in, heads, pj, c_in, stream, gu, e_in, h_all, part, f_out, f_in, acc, r_out, r_in
+        ) = buffers[h * PER_PART : (h + 1) * PER_PART]
+        for i in range(requests):
+            r = FIRST[h] + i
+            latent = dot(weights[r * 128 : (r + 1) * 128], keys[r][:, :KVL], nn)
+            o_out[:, i, :, :KVL] = latent.astype(BF).reshape(NT, 16, KVL)
+            o_out[:, i, :, KVL:] = parts[r * 128 : (r + 1) * 128].reshape(NT, 16, 128)
+        slot = links.reserve(NT)
+        for k in range(1, NT):
+            links.send(slot + k, o_out.at[t_to[k]], o_in.at[t], dp, t_to[k])
+        o_in[t] = o_out[t]
+        yield
+        for k in range(1, NT):
+            links.arrived(slot + k, o_in.at[t_from[k]], dp, t_from[k])
+        lse = [jnp.sum(o_in[s, :, :, KVL:].astype(F32), axis=2, keepdims=True) for s in range(NT)]
+        top = functools.reduce(jnp.maximum, lse)
+        shares = [jnp.exp(v - top) for v in lse]
+        total = functools.reduce(jnp.add, shares)
+        latent = jnp.zeros((requests, 16, KVL), F32)
+        for s in range(NT):
+            latent = latent + o_in[s, :, :, :KVL].astype(F32) * (shares[s] / total)
+        latent = latent.astype(BF).reshape(requests * 16, KVL)
+
+        head = rem(iota((requests * 16, 1), 0), 8)
+        values = jnp.zeros((requests * 16, HD), F32)
+        for i in range(8):
+            values = jnp.where(head == i, dot(latent, w_uv[i], nn), values)
+        row, col = iota((2 * padded, 1), 0), iota((2 * padded, requests * 16), 1)
+        inner = rem(row, padded)
+        at = div(inner, 4) * 8 + div(row, padded) * 4 + rem(inner, 4)
+        split = jnp.logical_and(inner < 4 * tokens, col == at).astype(BF)
+        ho[...] = dot(split, values.astype(BF), nn).astype(BF).reshape(2, padded, HD)
+
+        slot = links.reserve(NG)
+        for k in range(1, NG):
+            links.send(slot + k, ho.at[lax.rem(g_to[k], 2)], b_in.at[g], group(g_to[k]), t)
+        b_in[g] = ho[core]
+        yield
+        for k in range(1, NG):
+            links.arrived(slot + k, b_in.at[g_from[k]], group(g_from[k]), t)
+        row, col = iota((rows, 1), 0), iota((rows, NG * padded), 1)
+        at = div(row, tokens) * padded + rem(row, tokens) * 4
+        gathered = b_in[...].reshape(NG * padded, HD)
+        for i in range(4):
+            heads[core, y, :, i * HD : (i + 1) * HD] = dot((col == at + i).astype(BF), gathered, nn).astype(BF)
         yield from gather(heads, h)
 
         projected = dot(w_o[:, :KVL], heads[0].reshape(lanes, KVL), nt)
@@ -437,22 +452,23 @@
         links.arrived(slot, f_in, partner, t)
         acc[...] = (part[:, mine] + f_in[...].astype(F32)).reshape(NY, rows, KVL)
         value = yield from scatter(acc, r_out, r_in, h)
-        last[h * ROWS[0] : h * ROWS[0] + rows] = value.astype(BF)
+        last[FIRST[h] * 16 : FIRST[h] * 16 + rows] = value.astype(BF)
 
     place = jnp.logical_and(iota((16, 896), 1) == dp * 14 + iota((16, 896), 0), iota((16, 896), 0) < 14).astype(BF)
     mine = pl.ds(pl.multiple_of(core * 384, 128), KVL)
     other = pl.ds(pl.multiple_of((1 - core) * 384, 128), KVL)
-    gathered = b_in[...].reshape(128, KVL)
-    for h, rows in enumerate(ROWS):
-        row, col = iota((rows, 1), 0) + h * ROWS[0], iota((rows, 128), 1)
-        pack = (col == div(row, 10) * 16 + rem(row, 10)).astype(BF)
-        halves[h * PER_HALF + 1][core, y] = dot(pack, gathered, nn).astype(BF)
-    running = [chain(h) for h in range(len(ROWS))]
+    running = [chain(h) for h in range(len(PARTS))]
     while running:
         running = [steps for steps in running if next(steps, DONE) is not DONE]
 
     row, col = iota((128, 1), 0), iota((128, 80), 1)
-    spread = jnp.logical_and(rem(row, 16) < 10, col == (div(row, 16)) * 10 + rem(row, 16)).astype(BF)
+    token = rem(row, 16)
+    at = jnp.full((128, 1), -1, jnp.int32)
+    for h, requests in enumerate(PARTS):
+        inner = token - 2 * FIRST[h]
+        here = jnp.logical_and(inner >= 0, inner < 2 * requests)
+        at = jnp.where(here, FIRST[h] * 16 + div(row, 16) * (2 * requests) + inner, at)
+    spread = (col == at).astype(BF)
     g_out[...] = dot(spread, last[...], nn).astype(BF).reshape(NG, 16, KVL)
     slot = links.reserve(NG)
     for k in range(1, NG):
@@ -470,7 +486,7 @@
     links.finish()
 
 
-SLOTS = 8 * 8 + 2 * (2 * 15 + 3 * 8 + 4 + 1 + 7)
+SLOTS = 8 * 6 + len(PARTS) * (2 * 15 + 5 * 8 + 4 + 1 + 7)
 
 
 def layer(*operands):
@@ -489,18 +505,18 @@
         ((384, 896), BF),
         ((NT, REQ, 16, LAT), BF),
         ((REQ, KEYS, LAT), BF),
-        ((NT, REQ, 16, 640), BF),
-        ((NT, REQ, 16, 640), BF),
-        ((2, 16, KVL), BF),
-        ((NG, 16, KVL), BF),
         ((80, KVL), BF),
         ((NG, 16, KVL), BF),
         ((NG, 16, KVL), BF),
     ]
-    for rows in ROWS:
-        lanes = NY * rows
+    for requests, padded in zip(PARTS, HALF_ROWS):
+        rows, lanes = 16 * requests, 128 * requests
         scratch += [
             ((16, lanes), F32),
+            ((NT, requests, 16, 640), BF),
+            ((NT, requests, 16, 640), BF),
+            ((2, padded, HD), BF),
+            ((NG, padded, HD), BF),
             ((2, NY, rows, KVL), BF),
             ((NT, 16, lanes), BF),
             ((NT, 16, lanes), BF),
@@ -562,7 +578,7 @@
         w_uv,
         w_out.transpose(2, 1, 0).reshape(112, 1024),
         residual.reshape(TOK, 14).T,
-        norm_gain.reshape(1, 896),
+        norm_gain,
         w_gate.T,
         w_up.T,
         w_down,

time: 136 us -> 130 us (0.956)
  Pallas kernels: 133 us -> 128 us
    pallas_call x1, Pallas kernels: 133 us -> 128 us  [layer(): pl.pallas_call(kernel, out_shape=jax.ShapeDtypeStruct((10, 896), BF), in_...]
where the time goes in v5:
time: 130 us
  Pallas kernels  128 us (98%)
  local copies, waits for them, and re-layouts  1.36 us (1%)
    pallas_call x1, Pallas kernels, layer(): pl.pallas_call(kernel, out_shape=jax.ShapeDtypeStruct((10, 896), BF), in_...  128 us

profile of v5, /device:TPU:1, one launch (start us, length us, event | category | flops | bytes accessed | tf_op | source)
XLA Modules:
  0.0 129.6 jit_solution(15930068993360175065)
XLA Ops:
  0.0 128.2 %layer.1 = bf16[10,896]{1,0:T(8,128)(2,1)} custom-call(s32[5,13]{1,0:T(8,128)} %refs_0_.1, s32[5]{0:T(128)} %refs_1_.1, s32[1,84]{1,0:T(1,128)} %refs_2_.1, s32[1,84]{1,0:T(1,128)} %refs_3_.1, bf16[5,16,576]{2,1,0:T(8,128)(2,1)} %bitcast.14, bf16[1040,576]{1,0:T(8,128)(2,1)} %bitcast.10, bf16[10,576]{1,0:T(8,128)(2,1)} %refs_6_.1, ...), custom_call_target="tpu_custom_call" | custom-call | flops 3000000000 | bytes 10000000 | tf_op jit(solution)/shard_map/layer/pallas_call | solution.py:538
  128.2 1.4 %copy.16 = bf16[10,896]{1,0:T(8,128)(2,1)} copy(bf16[10,896]{1,0:T(8,128)(2,1)} %layer.1) | data formatting | bytes 35840

commit v6 on v5

--- a/solution.py
+++ b/solution.py
@@ -19,6 +19,7 @@
 NY = 8
 NG = 8
 NT = 8
+NX = 4
 KEYS = 32
 TOK = 640
 EPS = 1e-06
@@ -31,6 +32,7 @@
 FIRST = tuple(sum(PARTS[:h]) for h in range(len(PARTS)))
 PER_PART = 18
 HALF_ROWS = tuple(-(-8 * requests // 16) * 16 for requests in PARTS)
+SPANS = ((slice(0, 384), slice(384, 576)),)
 DONE = object()
 
 
@@ -90,9 +92,9 @@
         table, lengths, mig_page, mig_dest, q, pool, fresh, w_uv, w_out, res, gain, w_gate, w_up, w_down
     ) = held
     (
-    own, a_y1, a_y2, a_y3, a_y4, a_z1, a_z2, a_z3, a_z4, w_gu, w_o, w_d,
-    q_all, keys, last, g_out, g_in, *buffers, send_sems, recv_sems, load_sems,
+    own, w_gu, w_o, w_d, q_all, keys, last, g_out, g_in, *buffers, send_sems, recv_sems, load_sems,
     ) = rest
+    inbox, buffers = buffers[: 8 * len(SPANS)], buffers[8 * len(SPANS) :]
     loads = [pltpu.make_async_copy(*pair, load_sems.at[i]) for i, pair in enumerate(zip(operands, held))]
     for i in (5, 2, 3, 4, 8, 9, 13, 10, 11, 12, 6, 0, 1, 7):
         loads[i].start()
@@ -103,6 +105,9 @@
     links = Links(send_sems, recv_sems)
     t_to = [lax.rem(t + k, NT) for k in range(NT)]
     t_from = [lax.rem(t + NT - k, NT) for k in range(NT)]
+    z_lo, x = t // NX, lax.rem(t, NX)
+    x_to = [lax.rem(x + k, NX) for k in range(NX)]
+    x_from = [lax.rem(x + NX - k, NX) for k in range(NX)]
     g_to = [lax.rem(g + k, NG) for k in range(NG)]
     g_from = [lax.rem(g + NG - k, NG) for k in range(NG)]
     y_to = [lax.rem(y + k, NY) for k in range(NY)]
@@ -125,11 +130,8 @@
     for k in range(1, NY):
         pl.semaphore_signal(barrier, inc=1, device_id={"dp": dp_of(y_to[k]), "tp": t}, device_id_type=MESH)
 
-    for i in (5, 2, 3, 4):
+    for i in (2, 3):
         loads[i].wait()
-    row = iota((144, 1), 0)
-    column = (div(row, 2)) * PAGE + 2 * t + rem(row, 2)
-    own[...] = dot((column == iota((144, POOL * PAGE), 1)).astype(BF), pool[...], nn).astype(BF)
     row = iota((384, 1), 0)
     inner = rem(row, 6)
     entry = rem(iota((1, CAP * 28), 1), CAP)
@@ -141,20 +143,51 @@
         return (source == iota((384, 144), 1)).astype(BF)
 
     first, second = div(row, 48), div(rem(row, 48), 6)
-    a_y1[...] = dot(outgoing(first * NG + second), own[:, :384], nn).astype(BF).reshape(NY, 48, 384)
-    a_z1[...] = dot(outgoing(second * NG + first), own[:, 384:], nn).astype(BF).reshape(NG, 48, 192)
-    q_all[t] = q[...]
-
+    for_y, for_g = outgoing(first * NG + second), outgoing(second * NG + first)
+    row = iota((144, 1), 0)
+    column = (div(row, 2)) * PAGE + 2 * t + rem(row, 2)
+    two = (column == iota((144, POOL * PAGE), 1)).astype(BF)
+    row, col = iota((384, 1), 0), iota((384, 384), 1)
+    swap = (col == (div(rem(row, 48), 6)) * 48 + (div(row, 48)) * 6 + rem(row, 6)).astype(BF)
+    for i in (5, 4):
+        loads[i].wait()
+    own[...] = dot(two, pool[...], nn).astype(BF)
+
+    def exchange(span_y, span_z, y1, y2, y3, y4, z1, z2, z3, z4):
+        width_y, width_z = span_y.stop - span_y.start, span_z.stop - span_z.start
+        y1[...] = dot(for_y, own[:, span_y], nn).astype(BF).reshape(NY, 48, width_y)
+        z1[...] = dot(for_g, own[:, span_z], nn).astype(BF).reshape(NG, 48, width_z)
+        along_y, along_g = links.reserve(NY), links.reserve(NG)
+        for k in range(1, NY):
+            links.send(along_y + k, y1.at[y_to[k]], y2.at[y], dp_of(y_to[k]), t)
+            links.send(along_g + k, z1.at[g_to[k]], z2.at[g], group(g_to[k]), t)
+        y2[y] = y1[y]
+        z2[g] = z1[g]
+        yield
+        for k in range(1, NY):
+            links.arrived(along_y + k, y2.at[y_from[k]], dp_of(y_from[k]), t)
+            links.arrived(along_g + k, z2.at[g_from[k]], group(g_from[k]), t)
+        y3[...] = dot(swap, y2[...].reshape(384, width_y), nn).astype(BF).reshape(NG, 48, width_y)
+        z3[...] = dot(swap, z2[...].reshape(384, width_z), nn).astype(BF).reshape(NY, 48, width_z)
+        along_g, along_y = links.reserve(NG), links.reserve(NY)
+        for k in range(1, NY):
+            links.send(along_g + k, y3.at[g_to[k]], y4.at[g], group(g_to[k]), t)
+            links.send(along_y + k, z3.at[y_to[k]], z4.at[y], dp_of(y_to[k]), t)
+        y4[g] = y3[g]
+        z4[y] = z3[y]
+        yield
+        for k in range(1, NY):
+            links.arrived(along_g + k, y4.at[g_from[k]], group(g_from[k]), t)
+            links.arrived(along_y + k, z4.at[y_from[k]], dp_of(y_from[k]), t)
+
+    pages = [exchange(*spans, *inbox[8 * i : 8 * i + 8]) for i, spans in enumerate(SPANS)]
+    q_all[x] = q[...]
     pl.semaphore_wait(barrier, 21)
-    along_y, along_g = links.reserve(NY), links.reserve(NG)
-    for k in range(1, NY):
-        links.send(along_y + k, a_y1.at[y_to[k]], a_y2.at[y], dp_of(y_to[k]), t)
-        links.send(along_g + k, a_z1.at[g_to[k]], a_z2.at[g], group(g_to[k]), t)
-    to_heads = links.reserve(NT)
-    for k in range(1, NT):
-        links.send(to_heads + k, q_all.at[t], q_all.at[t], dp, t_to[k])
-    a_y2[y] = a_y1[y]
-    a_z2[g] = a_z1[g]
+    for steps in pages:
+        next(steps)
+    to_heads = links.reserve(NX)
+    for k in range(1, NX):
+        links.send(to_heads + k, q_all.at[x], q_all.at[x], dp, z_lo * NX + x_to[k])
 
     for i in (8, 9, 13, 10, 11, 12):
         loads[i].wait()
@@ -171,19 +204,8 @@
         values = dot(res[...], (row == at).astype(BF), nn)
         buffers[h * PER_PART][...] = jnp.concatenate([values, jnp.zeros((2, 64 * tokens), F32)], axis=0)
 
-    for k in range(1, NY):
-        links.arrived(along_y + k, a_y2.at[y_from[k]], dp_of(y_from[k]), t)
-        links.arrived(along_g + k, a_z2.at[g_from[k]], group(g_from[k]), t)
-    row, col = iota((384, 1), 0), iota((384, 384), 1)
-    swap = (col == (div(rem(row, 48), 6)) * 48 + (div(row, 48)) * 6 + rem(row, 6)).astype(BF)
-    a_y3[...] = dot(swap, a_y2[...].reshape(384, 384), nn).astype(BF).reshape(NG, 48, 384)
-    a_z3[...] = dot(swap, a_z2[...].reshape(384, 192), nn).astype(BF).reshape(NY, 48, 192)
-    along_g, along_y = links.reserve(NG), links.reserve(NY)
-    for k in range(1, NY):
-        links.send(along_g + k, a_y3.at[g_to[k]], a_y4.at[g], group(g_to[k]), t)
-        links.send(along_y + k, a_z3.at[y_to[k]], a_z4.at[y], dp_of(y_to[k]), t)
-    a_y4[g] = a_y3[g]
-    a_z4[y] = a_z3[y]
+    for steps in pages:
+        next(steps)
 
     row, col = iota((NT * 80, 1), 0), iota((NT * 80, 288), 1)
     slot = rem(row, 80)
@@ -199,9 +221,8 @@
     squares_at = jnp.logical_and(rem(iota((NT * 80, 1), 0), 80) == 36, rem(iota((1, 1024), 1), 16) >= 14)
     w_gu[...] = jnp.where(squares_at, 1.0, dot(rows, spread, nn)).astype(BF)
 
-    for k in range(1, NY):
-        links.arrived(along_g + k, a_y4.at[g_from[k]], group(g_from[k]), t)
-        links.arrived(along_y + k, a_z4.at[y_from[k]], dp_of(y_from[k]), t)
+    for steps in pages:
+        next(steps, DONE)
 
     for i in (6, 0, 1):
         loads[i].wait()
@@ -224,37 +245,54 @@
     from_z = (at == iota((REQ * KEYS, 384), 1)).astype(BF)
     at = jnp.where(jnp.logical_and(place >= 26, place < 28), 2 * request + place - 26, -1)
     from_fresh = (at == iota((REQ * KEYS, 2 * REQ), 1)).astype(BF)
-    low = dot(from_own, own[:, :384], nn) + dot(from_fresh, fresh[:, :384], nn)
-    high = dot(from_own, own[:, 384:], nn) + dot(from_fresh, fresh[:, 384:], nn)
-    low = low + dot(from_y, a_y4[...].reshape(384, 384), nn)
-    high = high + dot(from_z, a_z4[...].reshape(384, 192), nn)
-    keys[:, :, :384] = low.astype(BF).reshape(REQ, KEYS, 384)
-    keys[:, :, 384:] = high.astype(BF).reshape(REQ, KEYS, 192)
-    for k in range(1, NT):
-        links.arrived(to_heads + k, q_all.at[t_from[k]], dp, t_from[k])
-
-    scores = [dot(q_all[:, r].reshape(NT * 16, LAT), keys[r], nt) for r in range(REQ)]
-    scores = jnp.concatenate(scores, axis=0) * SCALE
-    row, col = iota((REQ * 128, 1), 0), iota((REQ * 128, KEYS), 1)
-    length = jnp.full((REQ * 128, 1), lengths[0], jnp.int32)
-    for r in range(1, REQ):
-        length = jnp.where(row >= r * 128, lengths[r], length)
-    cached = jnp.logical_and(col < 26, (div(col, 2)) * PAGE + 2 * t + rem(col, 2) < length)
-    newer = jnp.logical_and(jnp.logical_and(col >= 26, col <= 26 + rem(div(row, 8), 2)), t == 0)
-    live = jnp.logical_or(cached, newer)
-    scores = jnp.where(live, scores, DEAD)
-    top = jnp.max(scores, axis=1, keepdims=True)
-    weights = jnp.where(live, jnp.exp(scores - top), 0.0)
-    total = jnp.sum(weights, axis=1, keepdims=True)
-    some = total > 0.0
-    total = jnp.where(some, total, 1.0)
-    weights = (weights / total).astype(BF)
-    lse = jnp.where(some, top + jnp.log(total), DEAD)
-    high = lse.astype(BF).astype(F32)
-    middle = (lse - high).astype(BF).astype(F32)
-    low = lse - high - middle
-    lane = iota((REQ * 128, 128), 1)
-    parts = jnp.where(lane == 0, high, jnp.where(lane == 1, middle, jnp.where(lane == 2, low, 0.0))).astype(BF)
+    for i, spans in enumerate(SPANS):
+        arrived = inbox[8 * i + 3], inbox[8 * i + 7]
+        for span, source, found in zip(spans, (from_y, from_z), arrived):
+            width = span.stop - span.start
+            rows = dot(from_own, own[:, span], nn) + dot(from_fresh, fresh[:, span], nn)
+            rows = rows + dot(source, found[...].reshape(384, width), nn)
+            keys[z_lo, :, :, span] = rows.astype(BF).reshape(REQ, KEYS, width)
+    opposite = lax.rem(t + NX, NT)
+    to_opposite = links.reserve(len(PARTS))
+    for h, requests in enumerate(PARTS):
+        mine = keys.at[z_lo, FIRST[h] : FIRST[h] + requests]
+        links.send(to_opposite + h, mine, mine, dp, opposite)
+    for k in range(1, NX):
+        links.arrived(to_heads + k, q_all.at[x_from[k]], dp, opposite)
+
+    def attend(h):
+        requests = PARTS[h]
+        span = range(FIRST[h], FIRST[h] + requests)
+        links.arrived(to_opposite + h, keys.at[1 - z_lo, FIRST[h] : FIRST[h] + requests], dp, opposite)
+        held = [keys[:, r].reshape(2 * KEYS, LAT) for r in span]
+        scores = [dot(q_all[:, r].reshape(NX * 16, LAT), k, nt) for r, k in zip(span, held)]
+        scores = jnp.concatenate(scores, axis=0) * SCALE
+        row, col = iota((requests * 64, 1), 0), iota((1, 2 * KEYS), 1)
+        length = jnp.full((requests * 64, 1), lengths[FIRST[h]], jnp.int32)
+        for i in range(1, requests):
+            length = jnp.where(row >= i * 64, lengths[FIRST[h] + i], length)
+        place, source = rem(col, KEYS), div(col, KEYS) * NX + x
+        token = div(place, 2) * PAGE + 2 * source + rem(place, 2)
+        cached = jnp.logical_and(jnp.where(place < 26, token, MAXP * PAGE) < length, place < 26)
+        newest = jnp.where(source == 0, 26 + rem(div(row, 8), 2), 0)
+        newer = jnp.logical_and(place >= 26, place <= newest)
+        live = jnp.logical_or(cached, newer)
+        scores = jnp.where(live, scores, DEAD)
+        top = jnp.max(scores, axis=1, keepdims=True)
+        weights = jnp.where(live, jnp.exp(scores - top), 0.0)
+        total = jnp.sum(weights, axis=1, keepdims=True)
+        some = total > 0.0
+        total = jnp.where(some, total, 1.0)
+        weights = (weights / total).astype(BF)
+        lse = jnp.where(some, top + jnp.log(total), DEAD)
+        high = lse.astype(BF).astype(F32)
+        middle = (lse - high).astype(BF).astype(F32)
+        low = lse - high - middle
+        lane = iota((requests * 64, 128), 1)
+        parts = jnp.where(lane == 0, high, jnp.where(lane == 1, middle, jnp.where(lane == 2, low, 0.0))).astype(BF)
+        latent = [dot(weights[i * 64 : (i + 1) * 64], k[:, :KVL], nn) for i, k in enumerate(held)]
+        return latent, [parts[i * 64 : (i + 1) * 64] for i in range(requests)]
+
     loads[7].wait()
     partner = dp + 1 - 2 * core
 
@@ -337,24 +375,22 @@
         (
             res_h, o_out, o_in, ho, b_in, heads, pj, c_in, stream, gu, e_in, h_all, part, f_out, f_in, acc, r_out, r_in
         ) = buffers[h * PER_PART : (h + 1) * PER_PART]
-        for i in range(requests):
-            r = FIRST[h] + i
-            latent = dot(weights[r * 128 : (r + 1) * 128], keys[r][:, :KVL], nn)
-            o_out[:, i, :, :KVL] = latent.astype(BF).reshape(NT, 16, KVL)
-            o_out[:, i, :, KVL:] = parts[r * 128 : (r + 1) * 128].reshape(NT, 16, 128)
-        slot = links.reserve(NT)
-        for k in range(1, NT):
-            links.send(slot + k, o_out.at[t_to[k]], o_in.at[t], dp, t_to[k])
-        o_in[t] = o_out[t]
-        yield
-        for k in range(1, NT):
-            links.arrived(slot + k, o_in.at[t_from[k]], dp, t_from[k])
-        lse = [jnp.sum(o_in[s, :, :, KVL:].astype(F32), axis=2, keepdims=True) for s in range(NT)]
+        for i, (latent, lse) in enumerate(zip(*attend(h))):
+            o_out[:, i, :, :KVL] = latent.astype(BF).reshape(NX, 16, KVL)
+            o_out[:, i, :, KVL:] = lse.reshape(NX, 16, 128)
+        slot = links.reserve(NX)
+        for k in range(1, NX):
+            links.send(slot + k, o_out.at[x_to[k]], o_in.at[x], dp, z_lo * NX + x_to[k])
+        o_in[x] = o_out[x]
+        yield
+        for k in range(1, NX):
+            links.arrived(slot + k, o_in.at[x_from[k]], dp, opposite)
+        lse = [jnp.sum(o_in[s, :, :, KVL:].astype(F32), axis=2, keepdims=True) for s in range(NX)]
         top = functools.reduce(jnp.maximum, lse)
         shares = [jnp.exp(v - top) for v in lse]
         total = functools.reduce(jnp.add, shares)
         latent = jnp.zeros((requests, 16, KVL), F32)
-        for s in range(NT):
+        for s in range(NX):
             latent = latent + o_in[s, :, :, :KVL].astype(F32) * (shares[s] / total)
         latent = latent.astype(BF).reshape(requests * 16, KVL)
 
@@ -486,35 +522,30 @@
     links.finish()
 
 
-SLOTS = 8 * 6 + len(PARTS) * (2 * 15 + 5 * 8 + 4 + 1 + 7)
+SLOTS = 8 * 2 + len(SPANS) * 8 * 4 + len(PARTS) * (2 * 15 + 5 * 8 + 4 + 1 + 7)
 
 
 def layer(*operands):
     scratch = [
         ((144, LAT), BF),
-        ((NY, 48, 384), BF),
-        ((NY, 48, 384), BF),
-        ((NG, 48, 384), BF),
-        ((NG, 48, 384), BF),
-        ((NG, 48, 192), BF),
-        ((NG, 48, 192), BF),
-        ((NY, 48, 192), BF),
-        ((NY, 48, 192), BF),
         ((NT * 80, 1024), BF),
         ((128, 1024), BF),
         ((384, 896), BF),
-        ((NT, REQ, 16, LAT), BF),
-        ((REQ, KEYS, LAT), BF),
+        ((NX, REQ, 16, LAT), BF),
+        ((2, REQ, KEYS, LAT), BF),
         ((80, KVL), BF),
         ((NG, 16, KVL), BF),
         ((NG, 16, KVL), BF),
     ]
+    for spans in SPANS:
+        for span in spans:
+            scratch += [((8, 48, span.stop - span.start), BF)] * 4
     for requests, padded in zip(PARTS, HALF_ROWS):
         rows, lanes = 16 * requests, 128 * requests
         scratch += [
             ((16, lanes), F32),
-            ((NT, requests, 16, 640), BF),
-            ((NT, requests, 16, 640), BF),
+            ((NX, requests, 16, 640), BF),
+            ((NX, requests, 16, 640), BF),
             ((2, padded, HD), BF),
             ((NG, padded, HD), BF),
             ((2, NY, rows, KVL), BF),

time: 130 us -> 125 us (0.962)
  Pallas kernels: 128 us -> 123 us
    pallas_call x1, Pallas kernels: 128 us -> 123 us  [layer(): pl.pallas_call(kernel, out_shape=jax.ShapeDtypeStruct((10, 896), BF), in_...]
where the time goes in v6:
time: 125 us
  Pallas kernels  123 us (98%)
  local copies, waits for them, and re-layouts  1.36 us (1%)
    pallas_call x1, Pallas kernels, layer(): pl.pallas_call(kernel, out_shape=jax.ShapeDtypeStruct((10, 896), BF), in_...  123 us

profile of v6, /device:TPU:1, one launch (start us, length us, event | category | flops | bytes accessed | tf_op | source)
XLA Modules:
  0.0 124.6 jit_solution(6530762873735472558)
XLA Ops:
  0.0 123.2 %layer.1 = bf16[10,896]{1,0:T(8,128)(2,1)} custom-call(s32[5,13]{1,0:T(8,128)} %refs_0_.1, s32[5]{0:T(128)} %refs_1_.1, s32[1,84]{1,0:T(1,128)} %refs_2_.1, s32[1,84]{1,0:T(1,128)} %refs_3_.1, bf16[5,16,576]{2,1,0:T(8,128)(2,1)} %bitcast.14, bf16[1040,576]{1,0:T(8,128)(2,1)} %bitcast.10, bf16[10,576]{1,0:T(8,128)(2,1)} %refs_6_.1, ...), custom_call_target="tpu_custom_call" | custom-call | flops 3000000000 | bytes 10000000 | tf_op jit(solution)/shard_map/layer/pallas_call | solution.py:569
  123.2 1.4 %copy.16 = bf16[10,896]{1,0:T(8,128)(2,1)} copy(bf16[10,896]{1,0:T(8,128)(2,1)} %layer.1) | data formatting | bytes 35840

commit v7 on v6

--- a/solution.py
+++ b/solution.py
@@ -30,9 +30,9 @@
 DEAD = -1e30
 PARTS = (2, 3)
 FIRST = tuple(sum(PARTS[:h]) for h in range(len(PARTS)))
-PER_PART = 18
+PER_PART = 20
 HALF_ROWS = tuple(-(-8 * requests // 16) * 16 for requests in PARTS)
-SPANS = ((slice(0, 384), slice(384, 576)),)
+SPANS = ((slice(0, 256), slice(384, 512)), (slice(256, 384), slice(512, 576)))
 DONE = object()
 
 
@@ -92,7 +92,7 @@
         table, lengths, mig_page, mig_dest, q, pool, fresh, w_uv, w_out, res, gain, w_gate, w_up, w_down
     ) = held
     (
-    own, w_gu, w_o, w_d, q_all, keys, last, g_out, g_in, *buffers, send_sems, recv_sems, load_sems,
+    own, w_gu, w_o, w_d, q_all, keys, *buffers, send_sems, recv_sems, load_sems,
     ) = rest
     inbox, buffers = buffers[: 8 * len(SPANS)], buffers[8 * len(SPANS) :]
     loads = [pltpu.make_async_copy(*pair, load_sems.at[i]) for i, pair in enumerate(zip(operands, held))]
@@ -373,7 +373,7 @@
         rows, lanes = NG * tokens, 64 * tokens
         padded = HALF_ROWS[h]
         (
-            res_h, o_out, o_in, ho, b_in, heads, pj, c_in, stream, gu, e_in, h_all, part, f_out, f_in, acc, r_out, r_in
+            res_h, o_out, o_in, ho, b_in, heads, pj, c_in, stream, gu, e_in, h_all, part, f_out, f_in, acc, r_out, r_in, g_out, g_in
         ) = buffers[h * PER_PART : (h + 1) * PER_PART]
         for i, (latent, lse) in enumerate(zip(*attend(h))):
             o_out[:, i, :, :KVL] = latent.astype(BF).reshape(NX, 16, KVL)
@@ -488,41 +488,47 @@
         links.arrived(slot, f_in, partner, t)
         acc[...] = (part[:, mine] + f_in[...].astype(F32)).reshape(NY, rows, KVL)
         value = yield from scatter(acc, r_out, r_in, h)
-        last[FIRST[h] * 16 : FIRST[h] * 16 + rows] = value.astype(BF)
+        value = value.astype(BF)
+        row, col = iota((NG * padded, 1), 0), iota((NG * padded, rows), 1)
+        inner = rem(row, padded)
+        at = jnp.where(inner < 4 * tokens, div(row, padded) * tokens + div(inner, 4), -1)
+        spread = jnp.zeros((NG * padded, HD), F32)
+        for i in range(4):
+            chosen = jnp.logical_and(col == at, rem(inner, 4) == i).astype(BF)
+            spread = spread + dot(chosen, value[:, i * HD : (i + 1) * HD], nn)
+        g_out[...] = spread.astype(BF).reshape(NG, padded, HD)
+        slot = links.reserve(NG)
+        for k in range(1, NG):
+            links.send(slot + k, g_out.at[g_to[k]], g_in.at[g], group(g_to[k]), t)
+        g_in[g] = g_out[g]
+        yield
+        for k in range(1, NG):
+            links.arrived(slot + k, g_in.at[g_from[k]], group(g_from[k]), t)
+        row, col = iota((16, 1), 0), iota((16, padded), 1)
+        token = row - 2 * FIRST[h]
+        at = jnp.where(jnp.logical_and(token >= 0, token < tokens), token * 4, -8)
+        chosen = [(col == at + i).astype(BF) for i in range(4)]
+        blocks = []
+        for side in range(2):
+            total = g_in[side].astype(F32)
+            for s in range(1, 4):
+                total = total + g_in[2 * s + side].astype(F32)
+            blocks += [dot(c, total.astype(BF), nn) for c in chosen[side:]]
+        results.append(jnp.concatenate(blocks, axis=1))
 
     place = jnp.logical_and(iota((16, 896), 1) == dp * 14 + iota((16, 896), 0), iota((16, 896), 0) < 14).astype(BF)
     mine = pl.ds(pl.multiple_of(core * 384, 128), KVL)
     other = pl.ds(pl.multiple_of((1 - core) * 384, 128), KVL)
+    results = []
     running = [chain(h) for h in range(len(PARTS))]
     while running:
         running = [steps for steps in running if next(steps, DONE) is not DONE]
 
-    row, col = iota((128, 1), 0), iota((128, 80), 1)
-    token = rem(row, 16)
-    at = jnp.full((128, 1), -1, jnp.int32)
-    for h, requests in enumerate(PARTS):
-        inner = token - 2 * FIRST[h]
-        here = jnp.logical_and(inner >= 0, inner < 2 * requests)
-        at = jnp.where(here, FIRST[h] * 16 + div(row, 16) * (2 * requests) + inner, at)
-    spread = (col == at).astype(BF)
-    g_out[...] = dot(spread, last[...], nn).astype(BF).reshape(NG, 16, KVL)
-    slot = links.reserve(NG)
-    for k in range(1, NG):
-        links.send(slot + k, g_out.at[g_to[k]], g_in.at[g], group(g_to[k]), t)
-    g_in[g] = g_out[g]
-    for k in range(1, NG):
-        links.arrived(slot + k, g_in.at[g_from[k]], group(g_from[k]), t)
-    first = jnp.zeros((16, KVL), F32)
-    second = jnp.zeros((16, KVL), F32)
-    for s in range(4):
-        first = first + g_in[2 * s].astype(F32)
-        second = second + g_in[2 * s + 1].astype(F32)
-    out[:, :KVL] = first.astype(BF)[:10]
-    out[:, KVL:] = second.astype(BF)[:10, 128:]
+    out[...] = functools.reduce(jnp.add, results).astype(BF)[:10]
     links.finish()
 
 
-SLOTS = 8 * 2 + len(SPANS) * 8 * 4 + len(PARTS) * (2 * 15 + 5 * 8 + 4 + 1 + 7)
+SLOTS = 8 * 2 + len(SPANS) * 8 * 4 + len(PARTS) * (2 * 15 + 6 * 8 + 4 + 1 + 7)
 
 
 def layer(*operands):
@@ -533,9 +539,6 @@
         ((384, 896), BF),
         ((NX, REQ, 16, LAT), BF),
         ((2, REQ, KEYS, LAT), BF),
-        ((80, KVL), BF),
-        ((NG, 16, KVL), BF),
-        ((NG, 16, KVL), BF),
     ]
     for spans in SPANS:
         for span in spans:
@@ -561,6 +564,8 @@
             ((NY, rows, KVL), F32),
             ((7, rows, KVL), BF),
             ((7, rows, KVL), BF),
+            ((NG, padded, HD), BF),
+            ((NG, padded, HD), BF),
         ]
     vmem = pl.BlockSpec(memory_space=pltpu.VMEM)
     held = [

time: 125 us -> 123 us (0.984)
  Pallas kernels: 123 us -> 121 us
    pallas_call x1, Pallas kernels: 123 us -> 121 us  [layer(): pl.pallas_call(kernel, out_shape=jax.ShapeDtypeStruct((10, 896), BF), in_...]
where the time goes in v7:
time: 123 us
  Pallas kernels  121 us (98%)
  local copies, waits for them, and re-layouts  1.36 us (1%)
    pallas_call x1, Pallas kernels, layer(): pl.pallas_call(kernel, out_shape=jax.ShapeDtypeStruct((10, 896), BF), in_...  121 us

profile of v7, /device:TPU:1, one launch (start us, length us, event | category | flops | bytes accessed | tf_op | source)
XLA Modules:
  0.0 122.8 jit_solution(14401460076176232977)
XLA Ops:
  0.0 121.4 %layer.1 = bf16[10,896]{1,0:T(8,128)(2,1)} custom-call(s32[5,13]{1,0:T(8,128)} %refs_0_.1, s32[5]{0:T(128)} %refs_1_.1, s32[1,84]{1,0:T(1,128)} %refs_2_.1, s32[1,84]{1,0:T(1,128)} %refs_3_.1, bf16[5,16,576]{2,1,0:T(8,128)(2,1)} %bitcast.14, bf16[1040,576]{1,0:T(8,128)(2,1)} %bitcast.10, bf16[10,576]{1,0:T(8,128)(2,1)} %refs_6_.1, ...), custom_call_target="tpu_custom_call" | custom-call | flops 3000000000 | bytes 10000000 | tf_op jit(solution)/shard_map/layer/pallas_call | solution.py:574
  121.4 1.4 %copy.16 = bf16[10,896]{1,0:T(8,128)(2,1)} copy(bf16[10,896]{1,0:T(8,128)(2,1)} %layer.1) | data formatting | bytes 35840

commit v8 on v7

--- a/solution.py
+++ b/solution.py
@@ -327,10 +327,10 @@
             forward(far + 2, at_y(2), -2)
         pass_on(at_y(-2))
         pass_on(at_y(2))
+        yield
         for i, step in ((2, -1), (3, 1)):
             arrived(near + i, at_y(step))
             pass_on(at_y(step))
-        yield
         for i, step in ((0, -3), (1, 3), (2, 4)):
             arrived(far + i, at_y(step))
             pass_on(at_y(step))

time: 123 us -> 123 us (level)
  no operation moved by 1% of the time
where the time goes in v8:
time: 123 us
  Pallas kernels  122 us (99%)
  local copies, waits for them, and re-layouts  1.36 us (1%)
    pallas_call x1, Pallas kernels, layer(): pl.pallas_call(kernel, out_shape=jax.ShapeDtypeStruct((10, 896), BF), in_...  122 us

profile of v8, /device:TPU:1, one launch (start us, length us, event | category | flops | bytes accessed | tf_op | source)
XLA Modules:
  0.0 123.0 jit_solution(10804376907274770981)
XLA Ops:
  0.0 121.7 %layer.1 = bf16[10,896]{1,0:T(8,128)(2,1)} custom-call(s32[5,13]{1,0:T(8,128)} %refs_0_.1, s32[5]{0:T(128)} %refs_1_.1, s32[1,84]{1,0:T(1,128)} %refs_2_.1, s32[1,84]{1,0:T(1,128)} %refs_3_.1, bf16[5,16,576]{2,1,0:T(8,128)(2,1)} %bitcast.14, bf16[1040,576]{1,0:T(8,128)(2,1)} %bitcast.10, bf16[10,576]{1,0:T(8,128)(2,1)} %refs_6_.1, ...), custom_call_target="tpu_custom_call" | custom-call | flops 3000000000 | bytes 10000000 | tf_op jit(solution)/shard_map/layer/pallas_call | solution.py:574
  121.7 1.4 %copy.16 = bf16[10,896]{1,0:T(8,128)(2,1)} copy(bf16[10,896]{1,0:T(8,128)(2,1)} %layer.1) | data formatting | bytes 35840
